TPU v7x, 32 devices: a whole 2x2x4 slice. The times are simulated.
32 devices in a mesh: grp: 2 (over x), ma: 4 (over y, core), row: 4 (over z).
Axes of the slice: x: 2, y: 2, z: 4, core: 2. Of those that a mesh axis runs over, the one named last changes fastest.
Arguments:
- spectra: bfloat16 [512, 2, 513, 128], P(('grp', 'ma', 'row')), parts along dimension 0, may hold values from -6 to 6
- pair_low: int32 [256], replicated, may hold values from 0 to 255, each once
- legendre: bfloat16 [256, 513, 1024], P(('ma', 'row')), may hold values from -0.25 to 0.25
- dlegendre: bfloat16 [256, 513, 1024], P(('ma', 'row')), may hold values from -0.25 to 0.25
- base_flow: float32 [256, 1024], P(('grp', 'row'), 'ma'), parts along dimension 0, may hold values from -6 to 6
- lat_weights: float32 [1024], P('ma'), may hold values from 0.3 to 3
- to_eigen: bfloat16 [128, 128], replicated, may hold values from -0.5 to 0.5
- from_eigen: bfloat16 [128, 128], replicated, may hold values from -0.5 to 0.5
- decay_rates: float32 [128], replicated, may hold values from 0.1 to 10
Outputs:
- new_spectra: bfloat16 [512, 2, 513, 128], P(('grp', 'ma', 'row')), parts along dimension 0
There are 2 independent parts, one for each index of `grp`. A program takes and returns all parts, laid end to end along the dimension named above; an argument that names none is the same for every part. Nothing has to cross between parts.
Inputs may be any that keep to these rules, and one draw needn't show every extreme that they name: Pair p packs order pair_low[p] and order 512 - 1 - pair_low[p]; every value appears exactly once.
All inputs are finite; a program needn't handle non-finite values.
Results may differ from a plain program's by a relative error of at most 0.009.
Values may be sent and summed in bfloat16 or wider, within the bound.
No kernel may reach another device: no remote copies, remote signals or barrier semaphores. Data moves between devices by JAX's collectives and lax.ppermute only.
A program may use at most 384 MiB of HBM per device.

v0:
```python
import math

import jax
import jax.numpy as jnp
from jax import lax
from jax.sharding import PartitionSpec as P

time_step = 0.5
horizontal_scale = 4.0


def slot_layout(pair_low, n_slots):
    n_orders = n_slots - 1
    slot_ids = jnp.arange(n_slots, dtype=jnp.int32)
    low_side = slot_ids[None, :] < (n_orders - pair_low)[:, None]
    degree = jnp.where(low_side, pair_low[:, None] + slot_ids[None, :], slot_ids[None, :] - 1)
    order_masks = jnp.stack([low_side, jnp.logical_not(low_side)], axis=1)
    return (order_masks, degree)


def order_tables(pair_low, n_orders):
    n_lon = 2 * n_orders
    orders = jnp.stack([pair_low, n_orders - 1 - pair_low], axis=1)
    points = jnp.arange(n_lon, dtype=jnp.int32)
    phase_index = orders[:, :, None] * points[None, None, :] % n_lon
    radians = phase_index.astype(jnp.float32) * (2.0 * math.pi / n_lon)
    cosine_values = jnp.cos(radians)
    sine_values = jnp.sin(radians)
    stacked = jnp.stack([cosine_values, -sine_values], axis=2)
    synth_table = (stacked / math.sqrt(n_orders)).astype(jnp.bfloat16)
    analysis_table = (stacked / math.sqrt(n_lon)).astype(jnp.bfloat16)
    return (synth_table, analysis_table)


def on_device(
    spectra,
    pair_low,
    legendre,
    dlegendre,
    base_flow,
    lat_weights,
    to_eigen,
    from_eigen,
    decay_rates,
):
    pairs_here = spectra.shape[0]
    n_slots = spectra.shape[2]
    n_levels = spectra.shape[3]
    n_orders = n_slots - 1
    n_lat = legendre.shape[2]
    total_pairs = pair_low.shape[0]
    ma_count = lax.axis_size("ma")
    row_count = lax.axis_size("row")
    lat_here = n_lat // ma_count
    rad_here = n_levels // row_count
    cell_count = rad_here * lat_here
    first_pair = (lax.axis_index("ma") * row_count + lax.axis_index("row")) * pairs_here
    own_low = lax.dynamic_slice_in_dim(pair_low, first_pair, pairs_here)
    order_masks, degree = slot_layout(own_low, n_slots)
    order_flags = order_masks.astype(jnp.bfloat16)
    masked = order_flags[:, :, None, :, None] * spectra[:, None]
    masked = masked.reshape(pairs_here, 2, 2, n_slots, row_count, rad_here)
    leg_blocks = legendre.reshape(pairs_here, n_slots, ma_count, lat_here)
    slope_blocks = dlegendre.reshape(pairs_here, n_slots, ma_count, lat_here)
    main_lat = jnp.einsum(
        "pocsRr,psLl->LRpocrl", masked, leg_blocks, preferred_element_type=jnp.float32
    ).astype(jnp.bfloat16)
    slope_lat = jnp.einsum(
        "pocsRr,psLl->LRpocrl", masked, slope_blocks, preferred_element_type=jnp.float32
    ).astype(jnp.bfloat16)
    main_recv, slope_recv = (
        lax.all_to_all(
            main_lat.reshape(ma_count * row_count, pairs_here, 2, 2, cell_count),
            ("ma", "row"),
            split_axis=0,
            concat_axis=1,
            tiled=True,
        ),
        lax.all_to_all(
            slope_lat.reshape(ma_count * row_count, pairs_here, 2, 2, cell_count),
            ("ma", "row"),
            split_axis=0,
            concat_axis=1,
            tiled=True,
        ),
    )
    main_recv = main_recv.reshape(total_pairs, 2, 2, cell_count)
    slope_recv = slope_recv.reshape(total_pairs, 2, 2, cell_count)
    synth_table, analysis_table = order_tables(pair_low, n_orders)
    main_grid = jnp.einsum(
        "pocx,pocn->xn", main_recv, synth_table, preferred_element_type=jnp.float32
    )
    slope_grid = jnp.einsum(
        "pocx,pocn->xn", slope_recv, synth_table, preferred_element_type=jnp.float32
    )
    background = base_flow.reshape(cell_count)
    product = (main_grid * (slope_grid + background[:, None])).astype(jnp.bfloat16)
    weights = jnp.tile(lat_weights, rad_here)
    product_modes = jnp.einsum(
        "xn,pocn->pocx", product, analysis_table, preferred_element_type=jnp.float32
    )
    product_modes = (product_modes * weights).astype(jnp.bfloat16)
    returned = lax.all_to_all(
        product_modes.reshape(total_pairs, 2, 2, 1, cell_count),
        ("ma", "row"),
        split_axis=0,
        concat_axis=3,
        tiled=True,
    )
    returned = returned.reshape(pairs_here, 2, 2, ma_count, row_count, rad_here, lat_here)
    partial_coeffs = jnp.einsum(
        "pocLRrl,psLl->pocsRr", returned, leg_blocks, preferred_element_type=jnp.float32
    )
    partial_coeffs = partial_coeffs.reshape(pairs_here, 2, 2, n_slots, n_levels)
    nonlinear = jnp.sum(
        order_masks.astype(jnp.float32)[:, :, None, :, None] * partial_coeffs, axis=1
    )
    right_side = (spectra.astype(jnp.float32) + time_step * nonlinear).astype(jnp.bfloat16)
    eigen_coeffs = jnp.einsum(
        "pcsr,kr->pcsk", right_side, to_eigen, preferred_element_type=jnp.float32
    )
    degree_float = degree.astype(jnp.float32)
    factor = 1.0 + horizontal_scale * degree_float * (degree_float + 1.0) / float(
        n_orders * n_orders
    )
    factor = factor[:, :, None] + decay_rates[None, None, :]
    scaled = (eigen_coeffs / factor[:, None]).astype(jnp.bfloat16)
    result = jnp.einsum("pcsk,rk->pcsr", scaled, from_eigen, preferred_element_type=jnp.float32)
    return result.astype(jnp.bfloat16)


def solution(mesh):
    in_specs = (
        P(("grp", "ma", "row"), None, None, None),
        P(),
        P(("ma", "row"), None, None),
        P(("ma", "row"), None, None),
        P(("grp", "row"), "ma"),
        P("ma"),
        P(),
        P(),
        P(),
    )
    out_specs = P(("grp", "ma", "row"), None, None, None)
    return jax.shard_map(
        on_device, mesh=mesh, in_specs=in_specs, out_specs=out_specs, check_vma=False
    )
```

profile of v0, /device:TPU:0, one launch (start us, length us, event | category | flops | bytes accessed | tf_op | source)
XLA Modules:
  0.0 1427.2 jit_solution(172021043721290884)
XLA Ops:
  0.0 0.0 copy-start
  0.0 1.3 broadcast_subtract_fusion.1
  1.3 0.0 copy-start.5
  1.3 0.5 copy-done.5
  1.8 0.1 iota_compare_fusion.1
  1.9 30.9 %reshape.249 = bf16[16,513,4,256]{3,2,0,1:T(4,128)(2,1)} reshape(bf16[16,513,1024]{2,0,1:T(8,128)(2,1)} %param.11) | data formatting | bytes 33619968 | tf_op jit(solution)/shard_map/reshape | solution.py:63
  32.8 11.6 copy.78
  44.4 0.7 fusion.69
  45.1 38.1 %convert_bitcast_fusion.1 = bf16[4,4,16,2,2,32,256]{6,5,0,1,4,3,2:T(8,128)(2,1)} fusion(bf16[16,513,4,256,1,1,1]{3,2,0,1,6,5,4:T(4,128)(2,1)} %bitcast.113, bf16[16,2,513,4,32]{2,4,3,1,0:T(8,128)(2,1)} %bitcast.119, bf16[16,2,513]{2,1,0:T(2,128)(2,1)S(1)} %get-tuple-element.7), kind=kOutput, calls=%fused_computation.18 | convolution fusion | flops 8631910400 | bytes 37822528 | tf_op jit(solution)/shard_map/pocsRr,psLl->LRpocrl/dot_general | solution.py:65
  83.2 14.2 copy.80
  97.4 25.7 %reshape.250 = bf16[16,16,2,2,8192]{4,1,3,2,0:T(8,128)(2,1)} reshape(bf16[4,4,16,2,2,32,256]{6,5,2,4,3,1,0:T(8,128)(2,1)} %copy.80) | data formatting | bytes 33554432 | tf_op jit(solution)/shard_map/reshape | solution.py:73
  123.1 7.7 all-to-all-start
  130.7 30.9 %reshape.252 = bf16[16,513,4,256]{3,2,0,1:T(4,128)(2,1)} reshape(bf16[16,513,1024]{2,0,1:T(8,128)(2,1)} %param.12) | data formatting | bytes 33619968 | tf_op jit(solution)/shard_map/reshape | solution.py:64
  161.7 38.1 %convert_bitcast_fusion = bf16[4,4,16,2,2,32,256]{6,5,0,1,4,3,2:T(8,128)(2,1)} fusion(bf16[16,513,4,256,1,1,1]{3,2,0,1,6,5,4:T(4,128)(2,1)} %bitcast.115, bf16[16,2,513,4,32]{2,4,3,1,0:T(8,128)(2,1)} %bitcast.120, bf16[16,2,513]{2,1,0:T(2,128)(2,1)S(1)} %get-tuple-element.7), kind=kOutput, calls=%fused_computation.17 | convolution fusion | flops 8631910400 | bytes 37822528 | tf_op jit(solution)/shard_map/pocsRr,psLl->LRpocrl/dot_general | solution.py:68
  199.8 14.1 copy.84
  213.9 25.6 %reshape.253 = bf16[16,16,2,2,8192]{4,1,3,2,0:T(8,128)(2,1)} reshape(bf16[4,4,16,2,2,32,256]{6,5,2,4,3,1,0:T(8,128)(2,1)} %copy.84) | data formatting | bytes 33554432 | tf_op jit(solution)/shard_map/reshape | solution.py:80
  239.6 0.0 copy-start.8
  239.6 0.0 copy-start.3
  239.6 0.0 copy-start.4
  239.6 255.2 %all-to-all-done = bf16[16,16,2,2,8192]{4,1,3,2,0:T(8,128)(2,1)} async-done(((bf16[16,16,2,2,8192]{4,1,3,2,0:T(8,128)(2,1)}), bf16[16,16,2,2,8192]{4,1,3,2,0:T(8,128)(2,1)}, u32[]{:S(2)}, u32[]{:S(2)}) %all-to-all-start) | async-done | bytes 16777248 | tf_op jit(solution)/shard_map/all_to_all | solution.py:72
  494.8 5.6 all-to-all-start.1
  500.4 0.0 copy-done.8
  500.4 0.0 copy-done.3
  500.5 0.0 copy-done.4
  500.5 8.3 fusion.58
  508.8 0.0 copy-start.1
  508.9 14.7 %copy.81 = bf16[16,16,2,2,8192]{4,1,0,3,2:T(8,128)(2,1)} copy(bf16[16,16,2,2,8192]{4,1,3,2,0:T(8,128)(2,1)} %all-to-all-done) | data formatting | bytes 33554432 | tf_op jit(solution)/shard_map/all_to_all | solution.py:72
  523.5 0.0 copy-done.1
  523.5 25.5 %fusion.12 = f32[8192,1024,1,1]{1,0,3,2:T(8,128)} fusion(bf16[256,2,2,8192]{3,0,2,1:T(8,128)(2,1)} %bitcast.118, f32[256,2,1,1024]{3,0,1,2:T(8,128)S(1)} %get-tuple-element.10, f32[256,2,1,1024]{3,0,1,2:T(8,128)S(1)} %get-tuple-element.9), kind=kOutput, calls=%fused_computation.15 | convolution fusion | flops 17183014912 | bytes 54525952 | tf_op jit(solution)/shard_map/pocx,pocn->xn/dot_general | solution.py:90
  549.0 315.3 %all-to-all-done.1 = bf16[16,16,2,2,8192]{4,1,3,2,0:T(8,128)(2,1)} async-done(((bf16[16,16,2,2,8192]{4,1,3,2,0:T(8,128)(2,1)}), bf16[16,16,2,2,8192]{4,1,3,2,0:T(8,128)(2,1)}, u32[]{:S(2)}, u32[]{:S(2)}) %all-to-all-start.1) | async-done | bytes 16777248 | tf_op jit(solution)/shard_map/all_to_all | solution.py:79
  864.4 13.9 copy.85
  878.3 28.6 %fusion.81 = bf16[8192,1024,1,1]{1,0,3,2:T(8,128)(2,1)} fusion(f32[8192]{0:T(1024)S(1)} %bitcast.123, bf16[256,2,2,8192]{3,0,2,1:T(8,128)(2,1)} %bitcast.117, f32[8192,1024,1,1]{1,0,3,2:T(8,128)} %fusion.12, f32[256,2,1,1024]{3,0,1,2:T(8,128)} %copy-done.1, f32[256,2,1,1024]{3,0,1,2:T(8,128)S(1)} %get-tuple-element.9), kind=kOutput, calls=%fused_computation.12.clone.clone.clone.2 | convolution fusion | flops 17208180736 | bytes 71335936 | tf_op jit(solution)/shard_map/pocx,pocn->xn/dot_general | solution.py:93
  906.9 24.3 %fusion.14 = bf16[256,2,2,1,8192]{4,0,2,1,3:T(8,128)(2,1)} fusion(f32[8192]{0:T(1024)S(1)} %bitcast.122, f32[256,2,1,1024]{3,0,1,2:T(8,128)} %copy-done.1, f32[256,2,1,1024]{3,0,1,2:T(8,128)S(1)} %get-tuple-element.9, bf16[8192,1024,1,1]{1,0,3,2:T(8,128)(2,1)} %fusion.81), kind=kOutput, calls=%fused_computation.19 | convolution fusion | flops 17199792128 | bytes 37781504 | tf_op jit(solution)/shard_map/xn,pocn->pocx/dot_general | solution.py:99
  931.3 30.7 %copy.88 = bf16[256,2,2,1,8192]{4,2,1,3,0:T(2,128)(2,1)} copy(bf16[256,2,2,1,8192]{4,0,2,1,3:T(8,128)(2,1)} %fusion.14) | data formatting | bytes 33554432 | tf_op jit(solution)/shard_map/reshape | solution.py:104
  962.0 0.0 copy-start.6
  962.0 0.0 copy-start.7
  962.0 0.0 copy-start.9
  962.0 5.2 all-to-all-start.2
  967.2 0.0 copy-done.6
  967.2 0.0 copy-done.7
  967.2 0.1 multiply_add_fusion
  967.3 0.0 copy-done.9
  967.3 3.2 broadcast_add_fusion
  970.5 360.7 %all-to-all-done.2 = bf16[256,2,2,1,8192]{4,2,1,3,0:T(2,128)(2,1)} async-done(((bf16[256,2,2,1,8192]{4,2,1,3,0:T(2,128)(2,1)}), bf16[256,2,2,1,8192]{4,2,1,3,0:T(2,128)(2,1)}, u32[]{:S(2)}, u32[]{:S(2)}) %all-to-all-start.2) | async-done | bytes 16777248 | tf_op jit(solution)/shard_map/all_to_all | solution.py:103
  1331.2 14.7 %copy.89 = bf16[16,16,2,2,1,8192]{5,0,3,2,1,4:T(8,128)(2,1)S(1)} copy(bf16[16,16,2,2,1,8192]{5,3,2,1,0,4:T(2,128)(2,1)} %bitcast.19) | data formatting | bytes 33554432 | tf_op jit(solution)/shard_map/all_to_all | solution.py:103
  1346.0 0.0 copy-start.2
  1346.0 8.3 copy.122
  1354.3 0.0 copy-done.2
  1354.3 27.6 %fusion.2 = f32[16,2,4,32,513]{4,3,0,2,1:T(8,128)} fusion(f32[16,2,513]{2,1,0:T(2,128)S(1)} %copy-done.2, bf16[16,513,4,256,1,1,1]{3,2,0,1,6,5,4:T(4,128)(2,1)} %bitcast.114, bf16[16,2,2,4,4,32,256]{6,5,4,3,2,1,0:T(8,128)(2,1)} %bitcast.116), kind=kOutput, calls=%fused_computation.5 | convolution fusion | flops 8613015552 | bytes 42057856 | tf_op jit(solution)/shard_map/pocLRrl,psLl->pocsRr/dot_general | solution.py:111
  1382.0 5.3 multiply_bitcast_fusion
  1387.3 5.0 copy.93
  1392.3 10.7 copy.94
  1403.0 0.0 copy-start.10
  1403.0 7.4 add_convert_fusion
  1410.5 0.0 copy-done
  1410.5 0.0 copy-done.10
  1410.5 8.9 fusion.44
  1419.3 7.5 copy.96
  (6 shorter events, 0.1 us)
Async XLA Ops:
  0.0 1410.5 %copy-start = (bf16[128,128]{1,0:T(8,128)(2,1)S(1)}, bf16[128,128]{1,0:T(8,128)(2,1)}, u32[]{:S(2)}) copy-start(bf16[128,128]{1,0:T(8,128)(2,1)} %param.16) | copy-start | bytes 98308
  1.3 0.5 copy-start.5
  123.1 371.7 %all-to-all-start = ((bf16[16,16,2,2,8192]{4,1,3,2,0:T(8,128)(2,1)}), bf16[16,16,2,2,8192]{4,1,3,2,0:T(8,128)(2,1)}, u32[]{:S(2)}, u32[]{:S(2)}) async-start(bf16[16,16,2,2,8192]{4,1,3,2,0:T(8,128)(2,1)} %reshape.250), calls=%async_computation | async-start | bytes 33554432 | tf_op jit(solution)/shard_map/all_to_all | solution.py:72
  239.6 260.8 %copy-start.8 = (f32[256]{0:T(256)S(1)}, f32[256]{0:T(256)}, u32[]{:S(2)}) copy-start(f32[256]{0:T(256)} %param.14) | copy-start | bytes 3076
  239.6 260.9 %copy-start.3 = (f32[32,256]{1,0:T(8,128)S(1)}, f32[32,256]{1,0:T(8,128)}, u32[]{:S(2)}) copy-start(f32[32,256]{1,0:T(8,128)} %param.13) | copy-start | bytes 98308
  239.6 260.9 %copy-start.4 = (s32[256]{0:T(256)S(1)}, s32[256]{0:T(256)}, u32[]{:S(2)}) copy-start(s32[256]{0:T(256)} %param.10) | copy-start | bytes 3076
  494.8 369.6 %all-to-all-start.1 = ((bf16[16,16,2,2,8192]{4,1,3,2,0:T(8,128)(2,1)}), bf16[16,16,2,2,8192]{4,1,3,2,0:T(8,128)(2,1)}, u32[]{:S(2)}, u32[]{:S(2)}) async-start(bf16[16,16,2,2,8192]{4,1,3,2,0:T(8,128)(2,1)} %reshape.253), calls=%async_computation.1 | async-start | bytes 33554432 | tf_op jit(solution)/shard_map/all_to_all | solution.py:79
  508.8 14.7 %copy-start.1 = (f32[256,2,1,1024]{3,0,1,2:T(8,128)}, f32[256,2,1,1024]{3,0,1,2:T(8,128)S(1)}, u32[]{:S(2)}) copy-start(f32[256,2,1,1024]{3,0,1,2:T(8,128)S(1)} %get-tuple-element.10) | copy-start | bytes 6291460
  962.0 5.2 copy-start.6
  962.0 5.2 copy-start.7
  962.0 5.3 copy-start.9
  962.0 369.2 %all-to-all-start.2 = ((bf16[256,2,2,1,8192]{4,2,1,3,0:T(2,128)(2,1)}), bf16[256,2,2,1,8192]{4,2,1,3,0:T(2,128)(2,1)}, u32[]{:S(2)}, u32[]{:S(2)}) async-start(bf16[256,2,2,1,8192]{4,2,1,3,0:T(2,128)(2,1)} %copy.88), calls=%async_computation.2 | async-start | bytes 33554432 | tf_op jit(solution)/shard_map/all_to_all | solution.py:103
  1346.0 8.3 copy-start.2
  1403.0 7.4 copy-start.10
where the time goes:
time: 1440 us; the launch traced here: 1430 us
  waiting for transfers between devices  931 us (65%)
  local copies, waits for them, and re-layouts  259 us (18%)
  matrix products  191 us (13%)
  other arithmetic  26.5 us (2%)
  starting transfers between devices  18.4 us (1%)
    all_to_all x1, waiting for transfers between devices, on_device(): lax.all_to_all(product_modes.reshape(total_pairs, 2, 2, 1, cell_count), (...  361 us
    all_to_all x1, waiting for transfers between devices, on_device(): lax.all_to_all(slope_lat.reshape(ma_count * row_count, pairs_here, 2, 2,...  315 us
    all_to_all x1, waiting for transfers between devices, on_device(): lax.all_to_all(main_lat.reshape(ma_count * row_count, pairs_here, 2, 2, c...  255 us
    dot_general x1, matrix products, on_device(): jnp.einsum('pocsRr,psLl->LRpocrl', masked, slope_blocks, preferred_elemen...  38.1 us
    dot_general x1, matrix products, on_device(): jnp.einsum('pocsRr,psLl->LRpocrl', masked, leg_blocks, preferred_element_...  38.1 us
    reshape x1, local copies, waits for them, and re-layouts, on_device(): slope_blocks = dlegendre.reshape(pairs_here, n_slots, ma_count, lat_here)  30.9 us
    reshape x1, local copies, waits for them, and re-layouts, on_device(): leg_blocks = legendre.reshape(pairs_here, n_slots, ma_count, lat_here)  30.9 us
    reshape x1, local copies, waits for them, and re-layouts, on_device(): product_modes.reshape(total_pairs, 2, 2, 1, cell_count)  30.7 us
  transfers between devices with their start and end apart: 3, of which 3 were waited for; matrix products, arithmetic and copies ran while one was open for 11% of the time, Pallas kernels for 0%

commit v1 on v0

v1 whole, which is shorter than its diff:
```python
import functools
import math

import jax
import jax.numpy as jnp
from jax import lax
from jax.experimental import pallas as pl
from jax.experimental.pallas import tpu as pltpu
from jax.sharding import PartitionSpec as P

time_step = 0.5
horizontal_scale = 4.0
VMEM_BYTES = 56 * 2**20
MAIN_CUTS = (1, 3)
LAST_CUTS = (3, 1)


def params():
    return pltpu.CompilerParams(vmem_limit_bytes=VMEM_BYTES)


def cost(flops, nbytes):
    return pl.CostEstimate(flops=int(flops), bytes_accessed=int(nbytes), transcendentals=0)


def dot(a, b, a_dim=1, b_dim=0):
    return lax.dot_general(
        a, b, (((a_dim,), (b_dim,)), ((), ())), preferred_element_type=jnp.float32
    )


def split_orders(values, edge, half):
    n_orders = values.shape[0] - 1
    ids = lax.broadcasted_iota(jnp.int32, (n_orders, values.shape[1]), 0)
    body = values[0:n_orders]
    low = jnp.where(ids < edge, body, 0.0)
    high = jnp.where(ids[half:] >= edge, body[half:], 0.0)
    high = jnp.where(ids[half:] == half, values[n_orders:], high)
    return low.astype(jnp.bfloat16), high.astype(jnp.bfloat16)


def upper_rows(table_ref, p, half):
    n_orders = table_ref.shape[1] - 1
    upper = table_ref[p, half:n_orders].astype(jnp.float32)
    ids = lax.broadcasted_iota(jnp.int32, upper.shape, 0)
    last = table_ref[p, n_orders:].astype(jnp.float32)
    return jnp.where(ids == 0, last, upper).astype(jnp.bfloat16)


def synth_kernel(first, split, pos_ref, low_ref, s_ref, l_ref, *refs):
    outs, scratch = refs[-1 - split : -1], refs[-1]
    unit, _, n_slots, n_levels = s_ref.shape
    n_lat = l_ref.shape[2]
    n_orders = n_slots - 1
    half = n_orders // 2
    kl = 4 * unit
    for p in range(unit):
        edge = n_orders - low_ref[pos_ref[0] + first + pl.program_id(0) * unit + p]
        sides = [split_orders(s_ref[p, c].astype(jnp.float32), edge, half) for c in range(2)]
        results = (
            dot(l_ref[p, 0:n_orders], jnp.concatenate([sides[0][0], sides[1][0]], axis=1), 0, 0),
            dot(
                upper_rows(l_ref, p, half),
                jnp.concatenate([sides[0][1], sides[1][1]], axis=1),
                0,
                0,
            ),
        )
        for o in range(2):
            for c in range(2):
                start = p * 4 + o * 2 + c
                scratch[pl.ds(start, n_lat, stride=kl), :] = results[o][
                    :, c * n_levels : (c + 1) * n_levels
                ]
    n_dest, step = outs[0].shape[:2]
    for d in range(n_dest):
        for h in range(split):
            start = (d * split + h) * step * kl
            block = scratch[start : start + step * kl].astype(jnp.bfloat16)
            outs[h][d] = block.reshape(step, kl, n_levels)


def synthesize(pos, pair_low, spectra, table, first, count, unit, n_dest, split, after):
    _, _, n_slots, n_levels = spectra.shape
    n_lat = table.shape[2]
    lat_here = n_lat // n_dest
    kl = 4 * unit
    out_shape = (n_dest, lat_here // split, 4 * count, n_levels)
    at = first // unit
    flops = 2 * count * 2 * n_levels * n_slots * 1.5 * n_lat
    nbytes = 2 * (count * 2 * n_slots * n_levels + count * n_slots * n_lat + split * math.prod(out_shape))
    return pl.pallas_call(
        functools.partial(synth_kernel, first, split),
        grid_spec=pltpu.PrefetchScalarGridSpec(
            num_scalar_prefetch=2,
            grid=(count // unit,),
            in_specs=[
                pl.BlockSpec((unit, 2, n_slots, n_levels), lambda p, pos, low: (at + p, 0, 0, 0)),
                pl.BlockSpec((unit, n_slots, n_lat), lambda p, pos, low: (at + p, 0, 0)),
            ]
            + [pl.BlockSpec(memory_space=pl.ANY)] * len(after),
            out_specs=[
                pl.BlockSpec(
                    (n_dest, lat_here // split, kl, n_levels), lambda p, pos, low: (0, 0, p, 0)
                )
            ]
            * split,
            scratch_shapes=[pltpu.VMEM((n_lat * kl, n_levels), jnp.float32)],
        ),
        out_shape=[jax.ShapeDtypeStruct(out_shape, jnp.bfloat16)] * split,
        compiler_params=params(),
        cost_estimate=cost(flops, nbytes),
        name="synthesize",
    )(pos, pair_low, spectra, table, *after)


def gather_columns(refs):
    columns = []
    for t in range(refs[0].shape[1]):
        rows = [ref[:, t].reshape(-1, ref.shape[3]) for ref in refs]
        columns.append(jnp.concatenate(rows, axis=0))
    return jnp.concatenate(columns, axis=1)


def main_grid_kernel(table_ref, *refs):
    refs[-1][...] = dot(table_ref[...], gather_columns(refs[:-1]))


def product_kernel(table_ref, main_ref, base_ref, *refs):
    slope = dot(table_ref[...], gather_columns(refs[:-1]))
    refs[-1][...] = (main_ref[...] * (slope + base_ref[...])).astype(jnp.bfloat16)


def to_grid(table, chunks, main=None, base=None, part=0):
    n_lon, n_coeffs = table.shape
    lat_here, n_levels = chunks[0].shape[1], chunks[0].shape[3]
    step = min(4, lat_here)
    cells = lat_here * n_levels
    wide = pl.BlockSpec((n_lon, step * n_levels), lambda t: (0, t))
    skip = part * (lat_here // step)
    whole = pl.BlockSpec((n_lon, step * n_levels), lambda t: (0, skip + t))
    chunk_specs = [
        pl.BlockSpec((c.shape[0], step, c.shape[2], c.shape[3]), lambda t: (0, t, 0, 0))
        for c in chunks
    ]
    table_spec = pl.BlockSpec((n_lon, n_coeffs), lambda t: (0, 0))
    flops = 2 * n_lon * n_coeffs * cells
    if main is None:
        body, first_specs, first = main_grid_kernel, [table_spec], (table,)
        out_type = jnp.float32
    else:
        base_spec = pl.BlockSpec((1, step * n_levels), lambda t: (0, skip + t))
        body, first_specs, first = product_kernel, [table_spec, whole, base_spec], (table, main, base)
        out_type = jnp.bfloat16
    return pl.pallas_call(
        body,
        grid=(lat_here // step,),
        in_specs=first_specs + chunk_specs,
        out_specs=wide,
        out_shape=jax.ShapeDtypeStruct((n_lon, cells), out_type),
        compiler_params=params(),
        cost_estimate=cost(flops, 2 * n_coeffs * cells + 4 * n_lon * cells),
        name="to_grid",
    )(*first, *chunks)


def modes_kernel(table_ref, product_ref, weight_ref, *refs):
    out_ref, scratch = refs[-2:]
    n_dest, kl, step, n_levels = out_ref.shape
    rows = n_dest * kl
    modes = dot(table_ref[...], product_ref[...]) * weight_ref[...]
    for t in range(step):
        scratch[pl.ds(t, rows, stride=step), :] = modes[:, t * n_levels : (t + 1) * n_levels]
    out_ref[...] = scratch[...].astype(jnp.bfloat16).reshape(out_ref.shape)


def to_modes(table, product, weights, n_dest, n_levels, part, after):
    n_coeffs, n_lon = table.shape
    cells = product.shape[1]
    lat_here = cells // n_levels
    kl = n_coeffs // n_dest
    step = min(16, lat_here)
    skip = part * (lat_here // step)
    return pl.pallas_call(
        modes_kernel,
        grid=(lat_here // step,),
        in_specs=[
            pl.BlockSpec((n_coeffs, n_lon), lambda t: (0, 0)),
            pl.BlockSpec((n_lon, step * n_levels), lambda t: (0, t)),
            pl.BlockSpec((1, step * n_levels), lambda t: (0, skip + t)),
        ]
        + [pl.BlockSpec(memory_space=pl.ANY)] * len(after),
        out_specs=pl.BlockSpec((n_dest, kl, step, n_levels), lambda t: (0, 0, t, 0)),
        out_shape=jax.ShapeDtypeStruct((n_dest, kl, lat_here, n_levels), jnp.bfloat16),
        scratch_shapes=[pltpu.VMEM((n_coeffs * step, n_levels), jnp.float32)],
        compiler_params=params(),
        cost_estimate=cost(2 * n_coeffs * n_lon * cells, 2 * cells * (n_lon + n_coeffs)),
        name="to_modes",
    )(table, product, weights, *after)


def finish_kernel(
    first, split, pos_ref, low_ref, l_ref, s_ref, to_ref, from_ref, decay_ref, *refs
):
    m_refs, (out_ref, scratch) = refs[:split], refs[-2:]
    n_levels = m_refs[0].shape[3]
    n_lat = l_ref.shape[2]
    n_slots = l_ref.shape[1]
    n_orders = n_slots - 1
    half = n_orders // 2
    low = low_ref[pos_ref[0] + first + pl.program_id(0)]
    edge = n_orders - low
    sides = []
    for o in range(2):
        columns = []
        for c in range(2):
            parts = [m_ref[:, o * 2 + c] for m_ref in m_refs]
            columns.append(jnp.concatenate(parts, axis=1).reshape(n_lat, n_levels))
        sides.append(jnp.concatenate(columns, axis=1))
    one = dot(l_ref[0, 0:n_orders], sides[0])
    two = dot(upper_rows(l_ref, 0, half), sides[1])
    scratch[0:half] = one[0:half]
    ids = lax.broadcasted_iota(jnp.int32, two.shape, 0) + half
    scratch[half:n_orders] = jnp.where(ids < edge, one[half:], two)
    scratch[n_orders:n_slots] = two[0:1]
    slots = lax.broadcasted_iota(jnp.int32, (n_slots, 1), 0)
    degree = jnp.where(slots < edge, slots + low, slots - 1).astype(jnp.float32)
    factor = 1.0 + horizontal_scale * degree * (degree + 1.0) / float(n_orders * n_orders)
    factor = factor + decay_ref[...]
    for c in range(2):
        nonlinear = scratch[:, c * n_levels : (c + 1) * n_levels]
        right = s_ref[0, c].astype(jnp.float32) + time_step * nonlinear
        eigen = dot(right.astype(jnp.bfloat16), to_ref[...])
        scaled = (eigen / factor).astype(jnp.bfloat16)
        out_ref[0, c] = dot(scaled, from_ref[...]).astype(jnp.bfloat16)


def finish(pos, pair_low, modes, table, spectra, to_t, from_t, decay, first, count, out):
    n_slots, n_lat = table.shape[1:]
    n_levels = spectra.shape[3]
    mode_specs = [
        pl.BlockSpec(
            (x.shape[0], 4, x.shape[2], n_levels),
            functools.partial(lambda skip, p, pos, low: (0, skip + p, 0, 0), first - begin),
        )
        for begin, x in modes
    ]
    modes = [x for _, x in modes]
    pair_spec = pl.BlockSpec((1, 2, n_slots, n_levels), lambda p, pos, low: (first + p, 0, 0, 0))
    square = pl.BlockSpec((n_levels, n_levels), lambda p, pos, low: (0, 0))
    in_specs = [
        pl.BlockSpec((1, n_slots, n_lat), lambda p, pos, low: (first + p, 0, 0)),
        pair_spec,
        square,
        square,
        pl.BlockSpec((1, n_levels), lambda p, pos, low: (0, 0)),
        *mode_specs,
    ]
    operands = [table, spectra, to_t, from_t, decay, *modes]
    aliases = {}
    if out is not None:
        in_specs.append(pl.BlockSpec(memory_space=pl.ANY))
        operands.append(out)
        aliases = {len(operands) + 1: 0}
    flops = 2 * count * 2 * n_levels * n_slots * (1.5 * n_lat + 2 * n_levels)
    nbytes = 2 * (count * 4 * n_lat * n_levels + count * n_slots * (n_lat + 4 * n_levels))
    return pl.pallas_call(
        functools.partial(finish_kernel, first, len(modes)),
        grid_spec=pltpu.PrefetchScalarGridSpec(
            num_scalar_prefetch=2,
            grid=(count,),
            in_specs=in_specs,
            out_specs=pair_spec,
            scratch_shapes=[pltpu.VMEM((n_slots, 2 * n_levels), jnp.float32)],
        ),
        out_shape=jax.ShapeDtypeStruct(spectra.shape, jnp.bfloat16),
        input_output_aliases=aliases,
        compiler_params=params(),
        cost_estimate=cost(flops, nbytes),
        name="finish",
    )(pos, pair_low, *operands)


def order_tables(low, n_orders):
    n_lon = 2 * n_orders
    orders = jnp.stack([low, n_orders - 1 - low], axis=1)
    points = jnp.arange(n_lon, dtype=jnp.int32)
    phase_index = orders[:, :, None] * points[None, None, :] % n_lon
    radians = phase_index.astype(jnp.float32) * (2.0 * math.pi / n_lon)
    return jnp.stack([jnp.cos(radians), -jnp.sin(radians)], axis=2)


def cut_units(units, unit, sizes):
    if sum(sizes) != units:
        sizes = [units]
    ranges = []
    first = 0
    for size in sizes:
        ranges.append((first, size * unit))
        first += size * unit
    return ranges


def on_device(
    spectra,
    pair_low,
    legendre,
    dlegendre,
    base_flow,
    lat_weights,
    to_eigen,
    from_eigen,
    decay_rates,
):
    pairs_here, _, n_slots, n_levels = spectra.shape
    n_orders = n_slots - 1
    n_lat = legendre.shape[2]
    n_rows = lax.axis_size("row")
    n_dest = lax.axis_size("ma") * n_rows
    lat_here = n_lat // n_dest
    row = lax.axis_index("row")
    here = lax.axis_index("ma") * n_rows + row
    pos = (here * pairs_here).astype(jnp.int32).reshape(1)
    unit = min(4, pairs_here)
    units = pairs_here // unit
    main_cuts = cut_units(units, unit, MAIN_CUTS)
    last_cuts = cut_units(units, unit, LAST_CUTS)
    whole = [(0, pairs_here)]
    split = 2 if lat_here % 32 == 0 else 1

    def exchange(x):
        return lax.all_to_all(x, ("ma", "row"), split_axis=0, concat_axis=0, tiled=True)

    main_lat = []
    after = []
    for first, count in main_cuts:
        (lat,) = synthesize(
            pos, pair_low, spectra, legendre, first, count, unit, n_dest, 1, after
        )
        after = [lat]
        main_lat.append(exchange(lat))
    slopes = synthesize(
        pos, pair_low, spectra, dlegendre, 0, pairs_here, unit, n_dest, split, main_lat[:1]
    )
    slope_lat = [exchange(lat) for lat in slopes]

    table = order_tables(pair_low, n_orders).reshape(n_dest, pairs_here * 4, 2 * n_orders)
    synth_table = (table / math.sqrt(n_orders)).astype(jnp.bfloat16)
    analysis_table = (table / math.sqrt(2 * n_orders)).astype(jnp.bfloat16)

    def rows_of(which, ranges):
        parts = [
            which[:, 4 * f : 4 * (f + c)].reshape(-1, 2 * n_orders) for f, c in ranges
        ]
        return jnp.concatenate(parts, axis=0)

    base = lax.all_to_all(base_flow, "row", split_axis=1, concat_axis=0, tiled=True)
    base = base.T.reshape(1, lat_here * n_levels)
    weights = lax.dynamic_slice_in_dim(lat_weights, row * lat_here, lat_here)
    weights = jnp.repeat(weights, n_levels).reshape(1, lat_here * n_levels)

    main_grid = to_grid(rows_of(synth_table, main_cuts).T, main_lat)
    slope_table = rows_of(synth_table, whole).T
    arrived = []
    for part, lat in enumerate(slope_lat):
        product = to_grid(slope_table, [lat], main_grid, base, part)
        pieces = []
        for first, count in last_cuts if part == split - 1 else whole:
            rows = rows_of(analysis_table, [(first, count)])
            modes = to_modes(rows, product, weights, n_dest, n_levels, part, [])
            pieces.append((first, exchange(modes)))
        arrived.append(pieces)

    to_t, from_t, decay = to_eigen.T, from_eigen.T, decay_rates[None, :]
    out = None
    for n, (first, count) in enumerate(last_cuts):
        modes = [pieces[0] for pieces in arrived[:-1]] + [arrived[-1][n]]
        out = finish(
            pos,
            pair_low,
            modes,
            legendre,
            spectra,
            to_t,
            from_t,
            decay,
            first,
            count,
            out,
        )
    return out


def solution(mesh):
    in_specs = (
        P(("grp", "ma", "row"), None, None, None),
        P(),
        P(("ma", "row"), None, None),
        P(("ma", "row"), None, None),
        P(("grp", "row"), "ma"),
        P("ma"),
        P(),
        P(),
        P(),
    )
    out_specs = P(("grp", "ma", "row"), None, None, None)
    return jax.shard_map(
        on_device, mesh=mesh, in_specs=in_specs, out_specs=out_specs, check_vma=False
    )
```

time: 1440 us -> 1210 us (0.84)
  waiting for transfers between devices: 931 us -> 705 us
  matrix products: 191 us -> 0 us
  blocking collectives: 0 us -> 189 us
  local copies, waits for them, and re-layouts: 259 us -> 75.8 us
  Pallas kernels: 0 us -> 179 us
  starting transfers between devices: 18.4 us -> 36.5 us
    all_to_all x3 -> x7, waiting for transfers between devices: 931 us -> 705 us  [the longest x6 705 us: exchange(): lax.all_to_all(x, ('ma', 'row'), split_axis=0, concat_axis=0, tiled=True)]
    dot_general x7 -> x0, matrix products: 191 us -> none  [the longest x1 38.1 us: on_device(): jnp.einsum('pocsRr,psLl->LRpocrl', masked, slope_blocks, preferred_elemen...]
    all_to_all x0 -> x1, blocking collectives: none -> 189 us  [exchange(): lax.all_to_all(x, ('ma', 'row'), split_axis=0, concat_axis=0, tiled=True)]
    pallas_call x0 -> x11, Pallas kernels: none -> 179 us  [the longest x3 63.4 us: to_grid(): pl.pallas_call(body, grid=(lat_here // step,), in_specs=first_specs + chu...]
    reshape x5 -> x2, local copies, waits for them, and re-layouts: 144 us -> 1.81 us  [rows_of(): which[:, 4 * f:4 * (f + c)].reshape(-1, 2 * n_orders)]
    all_to_all x3, local copies, waits for them, and re-layouts: 43.4 us -> 1.42 us  [on_device(): lax.all_to_all(base_flow, 'row', split_axis=1, concat_axis=0, tiled=True)]
    unnamed x27 -> x17, local copies, waits for them, and re-layouts: 20.5 us -> 40 us
    all_to_all x3 -> x7, starting transfers between devices: 18.4 us -> 36.5 us  [the longest x6 30.1 us: exchange(): lax.all_to_all(x, ('ma', 'row'), split_axis=0, concat_axis=0, tiled=True)]
  transfers between devices with their start and end apart: 3 -> 7, of which waited for: 3 -> 6; matrix products, arithmetic and copies ran while one was open for 11% -> 7% of each run, Pallas kernels for 0% -> 14%
where the time goes in v1:
time: 1210 us; the launch traced here: 1200 us
  waiting for transfers between devices  705 us (58%)
  blocking collectives  189 us (16%)
  Pallas kernels  179 us (15%)
  local copies, waits for them, and re-layouts  75.8 us (6%)
  starting transfers between devices  36.5 us (3%)
  other arithmetic  14.1 us (1%)
    all_to_all x6, waiting for transfers between devices, exchange(): lax.all_to_all(x, ('ma', 'row'), split_axis=0, concat_axis=0, tiled=True)  705 us
    all_to_all x1, blocking collectives, exchange(): lax.all_to_all(x, ('ma', 'row'), split_axis=0, concat_axis=0, tiled=True)  189 us
    pallas_call x3, Pallas kernels, to_grid(): pl.pallas_call(body, grid=(lat_here // step,), in_specs=first_specs + chu...  63.4 us
    pallas_call x3, Pallas kernels, synthesize(): pl.pallas_call(functools.partial(synth_kernel, first, split), grid_spec=p...  48.3 us
    unnamed x17, local copies, waits for them, and re-layouts  40 us
    pallas_call x3, Pallas kernels, to_modes(): pl.pallas_call(modes_kernel, grid=(lat_here // step,), in_specs=[pl.Block...  39.3 us
    all_to_all x6, starting transfers between devices, exchange(): lax.all_to_all(x, ('ma', 'row'), split_axis=0, concat_axis=0, tiled=True)  30.1 us
    pallas_call x2, Pallas kernels, finish(): pl.pallas_call(functools.partial(finish_kernel, first, len(modes)), grid_...  28.4 us
  transfers between devices with their start and end apart: 7, of which 6 were waited for; matrix products, arithmetic and copies ran while one was open for 7% of the time, Pallas kernels for 14%

profile of v1, /device:TPU:0, one launch (start us, length us, event | category | flops | bytes accessed | tf_op | source)
XLA Modules:
  0.0 1200.2 jit_solution(16502805809048932593)
XLA Ops:
  0.0 0.8 all_to_all.37
  0.9 0.7 reshape.99
  1.6 6.3 all-to-all-start.2
  7.9 4.8 copy.87.s_ref
  12.7 15.8 %copy.86.l_ref = bf16[16,513,1024]{2,1,0:T(8,128)(2,1)} copy(bf16[16,513,1024]{2,0,1:T(8,128)(2,1)} %param.11) | data formatting | bytes 33619968 | tf_op args[2]
  28.5 9.2 synthesize.3.refs_0_
  37.7 0.0 all-to-all-done.2
  37.7 6.2 all-to-all-start
  43.9 17.5 %synthesize.4 = bf16[16,64,48,128]{3,2,1,0:T(8,128)(2,1)} custom-call(s32[1]{0:T(128)} %bitcast.pos_ref, s32[256]{0:T(256)} %low_ref.9, bf16[16,2,513,128]{3,2,1,0:T(8,128)(2,1)} %copy.87.s_ref, bf16[16,513,1024]{2,1,0:T(8,128)(2,1)} %copy.86.l_ref, bf16[16,64,16,128]{3,2,1,0:T(8,128)(2,1)} %synthesize.3.refs_0_), custom_call_target="tpu_custom_call" | custom-call | flops 4841275392 | bytes 28342272 | tf_op jit(solution)/shard_map/synthesize/pallas_call | solution.py:92
  61.5 76.9 %all-to-all-done.refs_0_ = bf16[16,64,16,128]{3,2,1,0:T(8,128)(2,1)} async-done(((bf16[16,64,16,128]{3,2,1,0:T(8,128)(2,1)}), bf16[16,64,16,128]{3,2,1,0:T(8,128)(2,1)}, u32[]{:S(2)}, u32[]{:S(2)}) %all-to-all-start) | async-done | bytes 4194336 | tf_op jit(solution)/shard_map/all_to_all | solution.py:332
  138.4 5.4 all-to-all-start.1
  143.8 15.8 %copy.82.l_ref = bf16[16,513,1024]{2,1,0:T(8,128)(2,1)} copy(bf16[16,513,1024]{2,0,1:T(8,128)(2,1)} %param.12) | data formatting | bytes 33619968 | tf_op args[3]
  159.6 21.6 %synthesize.5 = (bf16[16,32,64,128]{3,2,1,0:T(8,128)(2,1)}, bf16[16,32,64,128]{3,2,1,0:T(8,128)(2,1)}) custom-call(s32[1]{0:T(128)} %bitcast.pos_ref, s32[256]{0:T(256)} %low_ref.9, bf16[16,2,513,128]{3,2,1,0:T(8,128)(2,1)} %copy.87.s_ref, bf16[16,513,1024]{2,1,0:T(8,128)(2,1)} %copy.82.l_ref, bf16[16,64,16,128]{3,2,1,0:T(8,128)(2,1)} %all-to-all-done.refs_0_), custom_call_target="tpu_custom_call" | custom-call | flops 6455033856 | bytes 37789696 | tf_op jit(solution)/shard_map/synthesize/pallas_call | solution.py:92
  181.2 236.8 %all-to-all-done.1.refs_1_ = bf16[16,64,48,128]{3,2,1,0:T(8,128)(2,1)} async-done(((bf16[16,64,48,128]{3,2,1,0:T(8,128)(2,1)}), bf16[16,64,48,128]{3,2,1,0:T(8,128)(2,1)}, u32[]{:S(2)}, u32[]{:S(2)}) %all-to-all-start.1) | async-done | bytes 12582944 | tf_op jit(solution)/shard_map/all_to_all | solution.py:332
  418.0 189.1 %all_to_all.54.refs_0_ = bf16[16,32,64,128]{3,2,1,0:T(8,128)(2,1)} all-to-all(bf16[16,32,64,128]{3,2,1,0:T(8,128)(2,1)} %get-tuple-element.8), channel_id=1, replica_groups=mesh['grp'=2,'ma'=4,'row'=4] {'ma','row'}, dimensions={0} | all-to-all | bytes 16777216 | tf_op jit(solution)/shard_map/all_to_all | solution.py:332
  607.1 0.0 copy-start.1
  607.1 4.9 all-to-all-start.3
  612.0 0.0 copy-done.1
  612.0 8.3 fusion.6
  620.4 2.1 multiply_convert_fusion
  622.5 2.2 copy.70
  624.6 2.4 convert_element_type.39
  627.1 2.2 convert_element_type.38
  629.3 0.0 slice-start.1
  629.3 4.1 copy.71
  633.3 0.0 slice-start
  633.3 0.0 slice-done.1
  633.3 1.6 copy.74
  634.9 0.0 slice-done
  635.0 0.2 copy.73
  635.2 3.8 copy.69
  638.9 2.3 convert_element_type.40
  641.2 2.7 slice.19
  643.9 0.0 copy-done.4
  643.9 0.1 dynamic_slice.3
  644.0 2.9 maximum_bitcast_fusion.table_ref
  646.9 0.6 broadcast.102
  647.5 0.7 reduce
  648.2 0.1 reshape.100
  648.3 0.7 copy.80
  649.0 28.8 %to_grid.3.main_ref = f32[1024,8192]{1,0:T(8,128)} custom-call(bf16[1024,1024]{1,0:T(8,128)(2,1)} %maximum_bitcast_fusion.table_ref, bf16[16,64,16,128]{3,2,1,0:T(8,128)(2,1)} %all-to-all-done.refs_0_, bf16[16,64,48,128]{3,2,1,0:T(8,128)(2,1)} %all-to-all-done.1.refs_1_), custom_call_target="tpu_custom_call" | custom-call | flops 17179869184 | bytes 50331648 | tf_op jit(solution)/shard_map/to_grid/pallas_call | solution.py:155
  677.8 17.3 %to_grid.5.product_ref = bf16[1024,4096]{1,0:T(8,128)(2,1)} custom-call(bf16[1024,1024]{1,0:T(8,128)(2,1)} %bitcast.24, f32[1024,8192]{1,0:T(8,128)} %to_grid.3.main_ref, f32[1,8192]{1,0:T(1,128)} %bitcast.34, bf16[16,32,64,128]{3,2,1,0:T(8,128)(2,1)} %all_to_all.54.refs_0_), custom_call_target="tpu_custom_call" | custom-call | flops 8589934592 | bytes 25165824 | tf_op jit(solution)/shard_map/to_grid/pallas_call | solution.py:155
  695.1 0.7 broadcast_in_dim.9
  695.8 13.8 %to_modes.5 = bf16[16,48,32,128]{3,2,1,0:T(8,128)(2,1)} custom-call(bf16[768,1024]{1,0:T(8,128)(2,1)} %bitcast.29, bf16[1024,4096]{1,0:T(8,128)(2,1)} %to_grid.5.product_ref, f32[1,8192]{1,0:T(1,128)} %bitcast.38), custom_call_target="tpu_custom_call" | custom-call | flops 6442450944 | bytes 14680064 | tf_op jit(solution)/shard_map/to_modes/pallas_call | solution.py:184
  709.6 86.6 %all-to-all-done.3.refs_0_ = bf16[16,32,64,128]{3,2,1,0:T(8,128)(2,1)} async-done(((bf16[16,32,64,128]{3,2,1,0:T(8,128)(2,1)}), bf16[16,32,64,128]{3,2,1,0:T(8,128)(2,1)}, u32[]{:S(2)}, u32[]{:S(2)}) %all-to-all-start.3) | async-done | bytes 8388640 | tf_op jit(solution)/shard_map/all_to_all | solution.py:332
  796.3 4.9 all-to-all-start.7
  801.2 2.2 convert_element_type.36.table_ref
  803.4 17.3 %to_grid.4.product_ref = bf16[1024,4096]{1,0:T(8,128)(2,1)} custom-call(bf16[1024,1024]{1,0:T(8,128)(2,1)} %bitcast.25, f32[1024,8192]{1,0:T(8,128)} %to_grid.3.main_ref, f32[1,8192]{1,0:T(1,128)} %bitcast.35, bf16[16,32,64,128]{3,2,1,0:T(8,128)(2,1)} %all-to-all-done.3.refs_0_), custom_call_target="tpu_custom_call" | custom-call | flops 8589934592 | bytes 25165824 | tf_op jit(solution)/shard_map/to_grid/pallas_call | solution.py:155
  820.7 18.7 %to_modes.3 = bf16[16,64,32,128]{3,2,1,0:T(8,128)(2,1)} custom-call(bf16[1024,1024]{1,0:T(8,128)(2,1)} %convert_element_type.36.table_ref, bf16[1024,4096]{1,0:T(8,128)(2,1)} %to_grid.4.product_ref, f32[1,8192]{1,0:T(1,128)} %bitcast.39), custom_call_target="tpu_custom_call" | custom-call | flops 8589934592 | bytes 16777216 | tf_op jit(solution)/shard_map/to_modes/pallas_call | solution.py:184
  839.4 101.1 %all-to-all-done.7.refs_1_ = bf16[16,48,32,128]{3,2,1,0:T(8,128)(2,1)} async-done(((bf16[16,48,32,128]{3,2,1,0:T(8,128)(2,1)}), bf16[16,48,32,128]{3,2,1,0:T(8,128)(2,1)}, u32[]{:S(2)}, u32[]{:S(2)}) %all-to-all-start.7) | async-done | bytes 6291488 | tf_op jit(solution)/shard_map/all_to_all | solution.py:332
  940.5 4.8 all-to-all-start.4
  945.2 1.9 slice.18
  947.1 6.8 to_modes.4
  953.9 175.6 %all-to-all-done.4.refs_0_ = bf16[16,64,32,128]{3,2,1,0:T(8,128)(2,1)} async-done(((bf16[16,64,32,128]{3,2,1,0:T(8,128)(2,1)}), bf16[16,64,32,128]{3,2,1,0:T(8,128)(2,1)}, u32[]{:S(2)}, u32[]{:S(2)}) %all-to-all-start.4) | async-done | bytes 8388640 | tf_op jit(solution)/shard_map/all_to_all | solution.py:332
  1129.5 4.0 all-to-all-start.6
  1133.5 0.0 copy-done.2
  1133.5 0.7 copy.67
  1134.2 0.0 copy-done.3
  1134.2 0.7 copy.68
  1134.9 20.0 %finish.2.refs_2_ = bf16[16,2,513,128]{3,2,1,0:T(8,128)(2,1)} custom-call(s32[1]{0:T(128)} %bitcast.pos_ref, s32[256]{0:T(256)} %low_ref.9, bf16[16,513,1024]{2,1,0:T(8,128)(2,1)} %copy.86.l_ref, bf16[16,2,513,128]{3,2,1,0:T(8,128)(2,1)} %copy.87.s_ref, bf16[128,128]{1,0:T(8,128)(2,1)} %bitcast.30, bf16[128,128]{1,0:T(8,128)(2,1)} %bitcast.32, ...), custom_call_target="tpu_custom_call" | custom-call | flops 5648154624 | bytes 31494144 | tf_op jit(solution)/shard_map/finish/pallas_call | solution.py:267
  1155.0 27.9 %all-to-all-done.6.refs_1_ = bf16[16,16,32,128]{3,2,1,0:T(8,128)(2,1)S(1)} async-done(((bf16[16,16,32,128]{3,2,1,0:T(8,128)(2,1)}), bf16[16,16,32,128]{3,2,1,0:T(8,128)(2,1)S(1)}, u32[]{:S(2)}, u32[]{:S(2)}) %all-to-all-start.6) | async-done | bytes 2097184 | tf_op jit(solution)/shard_map/all_to_all | solution.py:332
  1182.9 1.3 copy-done
  1184.2 8.3 finish.3
  1192.5 7.5 copy.88
  (7 shorter events, 0.0 us)
Async XLA Ops:
  1.6 36.2 %all-to-all-start.2 = ((f32[4,1,2048]{2,1,0:T(1,128)}), f32[4,1,2048]{2,1,0:T(1,128)S(1)}, u32[]{:S(2)}, u32[]{:S(2)}) async-start(f32[4,1,2048]{2,1,0:T(1,128)} %reshape.99), calls=%async_computation.2 | async-start | bytes 65536 | tf_op jit(solution)/shard_map/all_to_all | solution.py:357
  37.7 100.7 %all-to-all-start = ((bf16[16,64,16,128]{3,2,1,0:T(8,128)(2,1)}), bf16[16,64,16,128]{3,2,1,0:T(8,128)(2,1)}, u32[]{:S(2)}, u32[]{:S(2)}) async-start(bf16[16,64,16,128]{3,2,1,0:T(8,128)(2,1)} %synthesize.3.refs_0_), calls=%async_computation | async-start | bytes 8388608 | tf_op jit(solution)/shard_map/all_to_all | solution.py:332
  138.4 279.6 %all-to-all-start.1 = ((bf16[16,64,48,128]{3,2,1,0:T(8,128)(2,1)}), bf16[16,64,48,128]{3,2,1,0:T(8,128)(2,1)}, u32[]{:S(2)}, u32[]{:S(2)}) async-start(bf16[16,64,48,128]{3,2,1,0:T(8,128)(2,1)} %synthesize.4), calls=%async_computation.1 | async-start | bytes 25165824 | tf_op jit(solution)/shard_map/all_to_all | solution.py:332
  607.1 4.9 copy-start.1
  607.1 189.1 %all-to-all-start.3 = ((bf16[16,32,64,128]{3,2,1,0:T(8,128)(2,1)}), bf16[16,32,64,128]{3,2,1,0:T(8,128)(2,1)}, u32[]{:S(2)}, u32[]{:S(2)}) async-start(bf16[16,32,64,128]{3,2,1,0:T(8,128)(2,1)} %get-tuple-element.7), calls=%async_computation.3 | async-start | bytes 16777216 | tf_op jit(solution)/shard_map/all_to_all | solution.py:332
  629.3 4.1 slice-start.1
  633.3 1.6 slice-start
  641.2 2.7 copy-start.4
  796.3 144.2 %all-to-all-start.7 = ((bf16[16,48,32,128]{3,2,1,0:T(8,128)(2,1)}), bf16[16,48,32,128]{3,2,1,0:T(8,128)(2,1)}, u32[]{:S(2)}, u32[]{:S(2)}) async-start(bf16[16,48,32,128]{3,2,1,0:T(8,128)(2,1)} %to_modes.5), calls=%async_computation.7 | async-start | bytes 12582912 | tf_op jit(solution)/shard_map/all_to_all | solution.py:332
  940.5 189.0 %all-to-all-start.4 = ((bf16[16,64,32,128]{3,2,1,0:T(8,128)(2,1)}), bf16[16,64,32,128]{3,2,1,0:T(8,128)(2,1)}, u32[]{:S(2)}, u32[]{:S(2)}) async-start(bf16[16,64,32,128]{3,2,1,0:T(8,128)(2,1)} %to_modes.3), calls=%async_computation.4 | async-start | bytes 16777216 | tf_op jit(solution)/shard_map/all_to_all | solution.py:332
  953.9 179.6 %copy-start.2 = (bf16[128,128]{1,0:T(8,128)(2,1)S(1)}, bf16[128,128]{1,0:T(8,128)(2,1)}, u32[]{:S(2)}) copy-start(bf16[128,128]{1,0:T(8,128)(2,1)} %param.15) | copy-start | bytes 98308
  953.9 180.3 %copy-start.3 = (bf16[128,128]{1,0:T(8,128)(2,1)S(1)}, bf16[128,128]{1,0:T(8,128)(2,1)}, u32[]{:S(2)}) copy-start(bf16[128,128]{1,0:T(8,128)(2,1)} %param.16) | copy-start | bytes 98308
  1129.5 53.4 %all-to-all-start.6 = ((bf16[16,16,32,128]{3,2,1,0:T(8,128)(2,1)}), bf16[16,16,32,128]{3,2,1,0:T(8,128)(2,1)S(1)}, u32[]{:S(2)}, u32[]{:S(2)}) async-start(bf16[16,16,32,128]{3,2,1,0:T(8,128)(2,1)} %to_modes.4), calls=%async_computation.6 | async-start | bytes 4194304 | tf_op jit(solution)/shard_map/all_to_all | solution.py:332
  1182.9 1.3 copy-start

commit v2 on v1

--- a/solution.py
+++ b/solution.py
@@ -111,6 +111,98 @@
         compiler_params=params(),
         cost_estimate=cost(flops, nbytes),
         name="synthesize",
+    )(pos, pair_low, spectra, table, *after)
+
+
+def tile_kernel(
+    first, split, unit, pos_ref, low_ref, s_ref, x_ref, *refs
+):
+    outs = refs[-4 - split : -4]
+    low_side, high_side, rows, scratch = refs[-4:]
+    _, _, n_slots, n_levels = s_ref.shape
+    n_orders = n_slots - 1
+    half = n_orders // 2
+    pairs, lanes = x_ref.shape[1:]
+    kl = 4 * unit
+    begin = first + pl.program_id(0) * unit
+    inside = lax.rem(begin, pairs)
+
+    @pl.when(pl.program_id(1) == 0)
+    def _():
+        for p in range(unit):
+            edge = n_orders - low_ref[pos_ref[0] + begin + p]
+            for c in range(2):
+                low, high = split_orders(s_ref[p, c].astype(jnp.float32), edge, half)
+                low_side[p, :, c * n_levels : (c + 1) * n_levels] = low
+                high_side[p, :, c * n_levels : (c + 1) * n_levels] = high
+
+    rows[...] = x_ref[...].astype(jnp.float32).reshape(n_slots * pairs, lanes)
+    ids = lax.broadcasted_iota(jnp.int32, (half, lanes), 0)
+    for p in range(unit):
+        body = rows[pl.ds(inside + p, n_orders, stride=pairs), :]
+        last = rows[pl.ds(n_orders * pairs + inside + p, 1), :]
+        upper = jnp.where(ids == 0, last, body[half:]).astype(jnp.bfloat16)
+        results = (
+            dot(body.astype(jnp.bfloat16), low_side[p], 0, 0),
+            dot(upper, high_side[p], 0, 0),
+        )
+        for o in range(2):
+            for c in range(2):
+                scratch[pl.ds(p * 4 + o * 2 + c, lanes, stride=kl), :] = results[o][
+                    :, c * n_levels : (c + 1) * n_levels
+                ]
+    n_dest, step = outs[0].shape[:2]
+    for d in range(n_dest):
+        for h in range(split):
+            start = (d * split + h) * step * kl
+            block = scratch[start : start + step * kl].astype(jnp.bfloat16)
+            outs[h][d] = block.reshape(step, kl, n_levels)
+
+
+def synthesize_tiles(pos, pair_low, spectra, table, first, count, unit, n_dest, split, after):
+    _, _, n_slots, n_levels = spectra.shape
+    n_lat = table.shape[2]
+    lat_here = n_lat // n_dest
+    lanes, pairs = 128, 8
+    n_orders = n_slots - 1
+    kl = 4 * unit
+    out_shape = (n_dest, lat_here // split, 4 * count, n_levels)
+    at = first // unit
+    flops = 2 * count * 2 * n_levels * n_slots * 1.5 * n_lat
+    nbytes = 2 * (count // unit * n_slots * pairs * n_lat + split * math.prod(out_shape))
+    return pl.pallas_call(
+        functools.partial(tile_kernel, first, split, unit),
+        grid_spec=pltpu.PrefetchScalarGridSpec(
+            num_scalar_prefetch=2,
+            grid=(count // unit, n_lat // lanes),
+            in_specs=[
+                pl.BlockSpec(
+                    (unit, 2, n_slots, n_levels), lambda u, t, pos, low: (at + u, 0, 0, 0)
+                ),
+                pl.BlockSpec(
+                    (n_slots, pairs, lanes),
+                    lambda u, t, pos, low: (0, (first + u * unit) // pairs, t),
+                ),
+            ]
+            + [pl.BlockSpec(memory_space=pl.ANY)] * len(after),
+            out_specs=[
+                pl.BlockSpec(
+                    (lanes // lat_here, lat_here // split, kl, n_levels),
+                    lambda u, t, pos, low: (t, 0, u, 0),
+                )
+            ]
+            * split,
+            scratch_shapes=[
+                pltpu.VMEM((unit, n_orders, 2 * n_levels), jnp.bfloat16),
+                pltpu.VMEM((unit, n_orders // 2, 2 * n_levels), jnp.bfloat16),
+                pltpu.VMEM((n_slots * pairs, lanes), jnp.float32),
+                pltpu.VMEM((lanes * kl, n_levels), jnp.float32),
+            ],
+        ),
+        out_shape=[jax.ShapeDtypeStruct(out_shape, jnp.bfloat16)] * split,
+        compiler_params=params(),
+        cost_estimate=cost(flops, nbytes),
+        name="synthesize_tiles",
     )(pos, pair_low, spectra, table, *after)
 
 
@@ -331,17 +423,28 @@
     def exchange(x):
         return lax.all_to_all(x, ("ma", "row"), split_axis=0, concat_axis=0, tiled=True)
 
+    tiles = pairs_here % 8 == 0 and 128 % lat_here == 0
+
+    def lat_functions(rows, first, count, parts, after):
+        if tiles:
+            body, rows = synthesize_tiles, jnp.transpose(rows, (1, 0, 2))
+        else:
+            body = synthesize
+        own = spectra
+        if first == 0 and count == unit:
+            own = lax.slice_in_dim(spectra, 0, unit)
+        return body(pos, pair_low, own, rows, first, count, unit, n_dest, parts, after)
+
     main_lat = []
     after = []
     for first, count in main_cuts:
-        (lat,) = synthesize(
-            pos, pair_low, spectra, legendre, first, count, unit, n_dest, 1, after
-        )
+        (lat,) = lat_functions(legendre, first, count, 1, after)
         after = [lat]
         main_lat.append(exchange(lat))
-    slopes = synthesize(
-        pos, pair_low, spectra, dlegendre, 0, pairs_here, unit, n_dest, split, main_lat[:1]
-    )
+    base = lax.all_to_all(base_flow, "row", split_axis=1, concat_axis=0, tiled=True)
+    base = base.T.reshape(1, lat_here * n_levels)
+
+    slopes = lat_functions(dlegendre, 0, pairs_here, split, after)
     slope_lat = [exchange(lat) for lat in slopes]
 
     table = order_tables(pair_low, n_orders).reshape(n_dest, pairs_here * 4, 2 * n_orders)
@@ -354,8 +457,6 @@
         ]
         return jnp.concatenate(parts, axis=0)
 
-    base = lax.all_to_all(base_flow, "row", split_axis=1, concat_axis=0, tiled=True)
-    base = base.T.reshape(1, lat_here * n_levels)
     weights = lax.dynamic_slice_in_dim(lat_weights, row * lat_here, lat_here)
     weights = jnp.repeat(weights, n_levels).reshape(1, lat_here * n_levels)
 

time: 1210 us -> 1200 us (level)
  waiting for transfers between devices: 705 us -> 391 us
  blocking collectives: 189 us -> 468 us
  Pallas kernels: 179 us -> 220 us
  local copies, waits for them, and re-layouts: 75.8 us -> 63.5 us
    all_to_all x6 -> x5, waiting for transfers between devices: 705 us -> 391 us  [exchange(): lax.all_to_all(x, ('ma', 'row'), split_axis=0, concat_axis=0, tiled=True)]
    all_to_all x1 -> x2, blocking collectives: 189 us -> 468 us  [exchange(): lax.all_to_all(x, ('ma', 'row'), split_axis=0, concat_axis=0, tiled=True)]
    pallas_call x3, Pallas kernels: 48.3 us -> 88.6 us  [synthesize_tiles(): pl.pallas_call(functools.partial(tile_kernel, first, split, unit), grid_s...]
    unnamed x17 -> x22, local copies, waits for them, and re-layouts: 40 us -> 24.1 us
    all_to_all x6 -> x5, starting transfers between devices: 30.1 us -> 25.2 us  [exchange(): lax.all_to_all(x, ('ma', 'row'), split_axis=0, concat_axis=0, tiled=True)]
  transfers between devices with their start and end apart: 7 -> 6, of which waited for: 6 -> 5; matrix products, arithmetic and copies ran while one was open for 7% -> 5% of each run, Pallas kernels for 14% -> 18%
where the time goes in v2:
time: 1200 us; the launch traced here: 1190 us
  blocking collectives  468 us (39%)
  waiting for transfers between devices  391 us (33%)
  Pallas kernels  220 us (18%)
  local copies, waits for them, and re-layouts  63.5 us (5%)
  starting transfers between devices  31.5 us (3%)
  other arithmetic  14.1 us (1%)
    all_to_all x2, blocking collectives, exchange(): lax.all_to_all(x, ('ma', 'row'), split_axis=0, concat_axis=0, tiled=True)  468 us
    all_to_all x5, waiting for transfers between devices, exchange(): lax.all_to_all(x, ('ma', 'row'), split_axis=0, concat_axis=0, tiled=True)  391 us
    pallas_call x3, Pallas kernels, synthesize_tiles(): pl.pallas_call(functools.partial(tile_kernel, first, split, unit), grid_s...  88.6 us
    pallas_call x3, Pallas kernels, to_grid(): pl.pallas_call(body, grid=(lat_here // step,), in_specs=first_specs + chu...  63.4 us
    pallas_call x3, Pallas kernels, to_modes(): pl.pallas_call(modes_kernel, grid=(lat_here // step,), in_specs=[pl.Block...  39.3 us
    pallas_call x2, Pallas kernels, finish(): pl.pallas_call(functools.partial(finish_kernel, first, len(modes)), grid_...  28.4 us
    all_to_all x5, starting transfers between devices, exchange(): lax.all_to_all(x, ('ma', 'row'), split_axis=0, concat_axis=0, tiled=True)  25.2 us
    unnamed x22, local copies, waits for them, and re-layouts  24.1 us
  transfers between devices with their start and end apart: 6, of which 5 were waited for; matrix products, arithmetic and copies ran while one was open for 5% of the time, Pallas kernels for 18%

profile of v2, /device:TPU:0, one launch (start us, length us, event | category | flops | bytes accessed | tf_op | source)
XLA Modules:
  0.0 1188.5 jit_solution(14234876244178016815)
XLA Ops:
  0.0 0.8 all_to_all.37
  0.9 0.7 reshape.99
  1.6 6.3 all-to-all-start.2
  7.9 2.7 copy.75.s_ref
  10.6 0.0 copy-start
  10.6 2.0 copy-done
  12.6 1.1 slice.22.s_ref
  13.7 12.3 %synthesize_tiles.3.refs_0_ = bf16[16,64,16,128]{3,2,1,0:T(8,128)(2,1)} custom-call(s32[1]{0:T(128)} %bitcast.pos_ref, s32[256]{0:T(256)} %low_ref.9, bf16[4,2,513,128]{3,2,1,0:T(8,128)(2,1)} %slice.22.s_ref, bf16[513,16,1024]{2,1,0:T(8,128)(2,1)} %bitcast.26), custom_call_target="tpu_custom_call" | custom-call | flops 1613758464 | bytes 12599296 | tf_op jit(solution)/shard_map/synthesize_tiles/pallas_call | solution.py:173
  26.0 0.0 all-to-all-done.2
  26.0 6.2 all-to-all-start
  32.2 33.1 %synthesize_tiles.4.refs_0_ = bf16[16,64,48,128]{3,2,1,0:T(8,128)(2,1)} custom-call(s32[1]{0:T(128)} %bitcast.pos_ref, s32[256]{0:T(256)} %low_ref.9, bf16[16,2,513,128]{3,2,1,0:T(8,128)(2,1)} %copy-done, bf16[513,16,1024]{2,1,0:T(8,128)(2,1)} %bitcast.27, bf16[16,64,16,128]{3,2,1,0:T(8,128)(2,1)} %synthesize_tiles.3.refs_0_), custom_call_target="tpu_custom_call" | custom-call | flops 4841275392 | bytes 37797888 | tf_op jit(solution)/shard_map/synthesize_tiles/pallas_call | solution.py:173
  65.4 43.2 %synthesize_tiles.5 = (bf16[16,32,64,128]{3,2,1,0:T(8,128)(2,1)}, bf16[16,32,64,128]{3,2,1,0:T(8,128)(2,1)}) custom-call(s32[1]{0:T(128)} %bitcast.pos_ref, s32[256]{0:T(256)} %low_ref.9, bf16[16,2,513,128]{3,2,1,0:T(8,128)(2,1)} %copy-done, bf16[513,16,1024]{2,1,0:T(8,128)(2,1)} %bitcast.30, bf16[16,64,48,128]{3,2,1,0:T(8,128)(2,1)} %synthesize_tiles.4.refs_0_), custom_call_target="tpu_custom_call" | custom-call | flops 6455033856 | bytes 50397184 | tf_op jit(solution)/shard_map/synthesize_tiles/pallas_call | solution.py:173
  108.6 18.1 %all-to-all-done.refs_0_ = bf16[16,64,16,128]{3,2,1,0:T(8,128)(2,1)} async-done(((bf16[16,64,16,128]{3,2,1,0:T(8,128)(2,1)}), bf16[16,64,16,128]{3,2,1,0:T(8,128)(2,1)}, u32[]{:S(2)}, u32[]{:S(2)}) %all-to-all-start) | async-done | bytes 4194336 | tf_op jit(solution)/shard_map/all_to_all | solution.py:424
  126.7 190.2 %all_to_all.54.refs_0_ = bf16[16,32,64,128]{3,2,1,0:T(8,128)(2,1)} all-to-all(bf16[16,32,64,128]{3,2,1,0:T(8,128)(2,1)} %get-tuple-element.8), channel_id=1, replica_groups=mesh['grp'=2,'ma'=4,'row'=4] {'ma','row'}, dimensions={0} | all-to-all | bytes 16777216 | tf_op jit(solution)/shard_map/all_to_all | solution.py:424
  316.9 0.0 copy-done.1
  316.9 278.0 %all_to_all.55.refs_1_ = bf16[16,64,48,128]{3,2,1,0:T(8,128)(2,1)} all-to-all(bf16[16,64,48,128]{3,2,1,0:T(8,128)(2,1)S(1)} %copy-done.1), channel_id=1, replica_groups=mesh['grp'=2,'ma'=4,'row'=4] {'ma','row'}, dimensions={0} | all-to-all | bytes 25165824 | tf_op jit(solution)/shard_map/all_to_all | solution.py:424
  594.9 5.4 all-to-all-start.3
  600.3 0.0 copy-done.4
  600.4 8.3 fusion.6
  608.7 2.1 multiply_convert_fusion
  610.8 2.2 copy.61
  613.0 2.4 convert_element_type.39
  615.4 2.8 slice.21
  618.1 2.2 convert_element_type.38
  620.4 2.8 copy.65
  623.1 0.0 slice-done
  623.1 0.2 copy.64
  623.3 0.0 copy-done.3
  623.3 2.6 copy.62
  625.9 3.7 copy.60
  629.6 2.3 convert_element_type.40
  632.0 2.8 slice.24
  634.8 0.0 copy-done.7
  634.8 0.1 dynamic_slice.3
  634.8 2.9 maximum_bitcast_fusion.table_ref
  637.8 0.5 broadcast.102
  638.3 0.7 reduce
  639.0 0.1 reshape.100
  639.1 0.7 copy.69
  639.8 28.8 %to_grid.3.main_ref = f32[1024,8192]{1,0:T(8,128)} custom-call(bf16[1024,1024]{1,0:T(8,128)(2,1)} %maximum_bitcast_fusion.table_ref, bf16[16,64,16,128]{3,2,1,0:T(8,128)(2,1)} %all-to-all-done.refs_0_, bf16[16,64,48,128]{3,2,1,0:T(8,128)(2,1)} %all_to_all.55.refs_1_), custom_call_target="tpu_custom_call" | custom-call | flops 17179869184 | bytes 50331648 | tf_op jit(solution)/shard_map/to_grid/pallas_call | solution.py:247
  668.6 17.3 %to_grid.5.product_ref = bf16[1024,4096]{1,0:T(8,128)(2,1)} custom-call(bf16[1024,1024]{1,0:T(8,128)(2,1)} %bitcast.28, f32[1024,8192]{1,0:T(8,128)} %to_grid.3.main_ref, f32[1,8192]{1,0:T(1,128)} %bitcast.39, bf16[16,32,64,128]{3,2,1,0:T(8,128)(2,1)} %all_to_all.54.refs_0_), custom_call_target="tpu_custom_call" | custom-call | flops 8589934592 | bytes 25165824 | tf_op jit(solution)/shard_map/to_grid/pallas_call | solution.py:247
  685.9 0.7 broadcast_in_dim.9
  686.6 13.9 %to_modes.5 = bf16[16,48,32,128]{3,2,1,0:T(8,128)(2,1)} custom-call(bf16[768,1024]{1,0:T(8,128)(2,1)} %bitcast.34, bf16[1024,4096]{1,0:T(8,128)(2,1)} %to_grid.5.product_ref, f32[1,8192]{1,0:T(1,128)} %bitcast.43), custom_call_target="tpu_custom_call" | custom-call | flops 6442450944 | bytes 14680064 | tf_op jit(solution)/shard_map/to_modes/pallas_call | solution.py:276
  700.5 84.1 %all-to-all-done.3.refs_0_ = bf16[16,32,64,128]{3,2,1,0:T(8,128)(2,1)} async-done(((bf16[16,32,64,128]{3,2,1,0:T(8,128)(2,1)}), bf16[16,32,64,128]{3,2,1,0:T(8,128)(2,1)}, u32[]{:S(2)}, u32[]{:S(2)}) %all-to-all-start.3) | async-done | bytes 8388640 | tf_op jit(solution)/shard_map/all_to_all | solution.py:424
  784.6 4.9 all-to-all-start.7
  789.5 2.2 convert_element_type.36.table_ref
  791.7 17.3 %to_grid.4.product_ref = bf16[1024,4096]{1,0:T(8,128)(2,1)} custom-call(bf16[1024,1024]{1,0:T(8,128)(2,1)} %bitcast.29, f32[1024,8192]{1,0:T(8,128)} %to_grid.3.main_ref, f32[1,8192]{1,0:T(1,128)} %bitcast.40, bf16[16,32,64,128]{3,2,1,0:T(8,128)(2,1)} %all-to-all-done.3.refs_0_), custom_call_target="tpu_custom_call" | custom-call | flops 8589934592 | bytes 25165824 | tf_op jit(solution)/shard_map/to_grid/pallas_call | solution.py:247
  809.0 18.7 %to_modes.3 = bf16[16,64,32,128]{3,2,1,0:T(8,128)(2,1)} custom-call(bf16[1024,1024]{1,0:T(8,128)(2,1)} %convert_element_type.36.table_ref, bf16[1024,4096]{1,0:T(8,128)(2,1)} %to_grid.4.product_ref, f32[1,8192]{1,0:T(1,128)} %bitcast.44), custom_call_target="tpu_custom_call" | custom-call | flops 8589934592 | bytes 16777216 | tf_op jit(solution)/shard_map/to_modes/pallas_call | solution.py:276
  827.7 101.1 %all-to-all-done.7.refs_1_ = bf16[16,48,32,128]{3,2,1,0:T(8,128)(2,1)} async-done(((bf16[16,48,32,128]{3,2,1,0:T(8,128)(2,1)}), bf16[16,48,32,128]{3,2,1,0:T(8,128)(2,1)}, u32[]{:S(2)}, u32[]{:S(2)}) %all-to-all-start.7) | async-done | bytes 6291488 | tf_op jit(solution)/shard_map/all_to_all | solution.py:424
  928.8 4.7 all-to-all-start.4
  933.5 1.9 slice.23
  935.4 6.8 to_modes.4
  942.2 175.6 %all-to-all-done.4.refs_0_ = bf16[16,64,32,128]{3,2,1,0:T(8,128)(2,1)} async-done(((bf16[16,64,32,128]{3,2,1,0:T(8,128)(2,1)}), bf16[16,64,32,128]{3,2,1,0:T(8,128)(2,1)}, u32[]{:S(2)}, u32[]{:S(2)}) %all-to-all-start.4) | async-done | bytes 8388640 | tf_op jit(solution)/shard_map/all_to_all | solution.py:424
  1117.8 4.0 all-to-all-start.6
  1121.8 0.0 copy-start.5
  1121.8 0.0 copy-start.6
  1121.8 15.8 %copy.74.l_ref = bf16[16,513,1024]{2,1,0:T(8,128)(2,1)} copy(bf16[16,513,1024]{2,0,1:T(8,128)(2,1)} %param.11) | data formatting | bytes 33619968 | tf_op args[2]
  1137.6 0.7 copy.58
  1138.3 0.7 copy.59
  1139.0 20.0 %finish.2.refs_2_ = bf16[16,2,513,128]{3,2,1,0:T(8,128)(2,1)} custom-call(s32[1]{0:T(128)} %bitcast.pos_ref, s32[256]{0:T(256)} %low_ref.9, bf16[16,513,1024]{2,1,0:T(8,128)(2,1)} %copy.74.l_ref, bf16[16,2,513,128]{3,2,1,0:T(8,128)(2,1)} %copy-done, bf16[128,128]{1,0:T(8,128)(2,1)} %bitcast.35, bf16[128,128]{1,0:T(8,128)(2,1)} %bitcast.37, ...), custom_call_target="tpu_custom_call" | custom-call | flops 5648154624 | bytes 31494144 | tf_op jit(solution)/shard_map/finish/pallas_call | solution.py:359
  1159.1 12.1 %all-to-all-done.6.refs_1_ = bf16[16,16,32,128]{3,2,1,0:T(8,128)(2,1)S(1)} async-done(((bf16[16,16,32,128]{3,2,1,0:T(8,128)(2,1)}), bf16[16,16,32,128]{3,2,1,0:T(8,128)(2,1)S(1)}, u32[]{:S(2)}, u32[]{:S(2)}) %all-to-all-start.6) | async-done | bytes 2097184 | tf_op jit(solution)/shard_map/all_to_all | solution.py:424
  1171.1 1.3 copy-done.2
  1172.5 8.3 finish.3
  1180.8 7.5 copy.76
  (11 shorter events, 0.0 us)
Async XLA Ops:
  1.6 24.5 %all-to-all-start.2 = ((f32[4,1,2048]{2,1,0:T(1,128)}), f32[4,1,2048]{2,1,0:T(1,128)S(1)}, u32[]{:S(2)}, u32[]{:S(2)}) async-start(f32[4,1,2048]{2,1,0:T(1,128)} %reshape.99), calls=%async_computation.2 | async-start | bytes 65536 | tf_op jit(solution)/shard_map/all_to_all | solution.py:444
  10.6 2.0 copy-start
  26.0 100.7 %all-to-all-start = ((bf16[16,64,16,128]{3,2,1,0:T(8,128)(2,1)}), bf16[16,64,16,128]{3,2,1,0:T(8,128)(2,1)}, u32[]{:S(2)}, u32[]{:S(2)}) async-start(bf16[16,64,16,128]{3,2,1,0:T(8,128)(2,1)} %synthesize_tiles.3.refs_0_), calls=%async_computation | async-start | bytes 8388608 | tf_op jit(solution)/shard_map/all_to_all | solution.py:424
  126.7 190.2 %copy-start.1 = (bf16[16,64,48,128]{3,2,1,0:T(8,128)(2,1)S(1)}, bf16[16,64,48,128]{3,2,1,0:T(8,128)(2,1)}, u32[]{:S(2)}) copy-start(bf16[16,64,48,128]{3,2,1,0:T(8,128)(2,1)} %synthesize_tiles.4.refs_0_) | copy-start | bytes 37748740
  594.9 5.4 copy-start.4
  594.9 189.7 %all-to-all-start.3 = ((bf16[16,32,64,128]{3,2,1,0:T(8,128)(2,1)}), bf16[16,32,64,128]{3,2,1,0:T(8,128)(2,1)}, u32[]{:S(2)}, u32[]{:S(2)}) async-start(bf16[16,32,64,128]{3,2,1,0:T(8,128)(2,1)} %get-tuple-element.7), calls=%async_computation.3 | async-start | bytes 16777216 | tf_op jit(solution)/shard_map/all_to_all | solution.py:424
  620.3 2.8 slice-start
  620.4 3.0 copy-start.3
  632.0 2.8 copy-start.7
  784.6 144.2 %all-to-all-start.7 = ((bf16[16,48,32,128]{3,2,1,0:T(8,128)(2,1)}), bf16[16,48,32,128]{3,2,1,0:T(8,128)(2,1)}, u32[]{:S(2)}, u32[]{:S(2)}) async-start(bf16[16,48,32,128]{3,2,1,0:T(8,128)(2,1)} %to_modes.5), calls=%async_computation.7 | async-start | bytes 12582912 | tf_op jit(solution)/shard_map/all_to_all | solution.py:424
  928.8 189.0 %all-to-all-start.4 = ((bf16[16,64,32,128]{3,2,1,0:T(8,128)(2,1)}), bf16[16,64,32,128]{3,2,1,0:T(8,128)(2,1)}, u32[]{:S(2)}, u32[]{:S(2)}) async-start(bf16[16,64,32,128]{3,2,1,0:T(8,128)(2,1)} %to_modes.3), calls=%async_computation.4 | async-start | bytes 16777216 | tf_op jit(solution)/shard_map/all_to_all | solution.py:424
  1117.8 53.4 %all-to-all-start.6 = ((bf16[16,16,32,128]{3,2,1,0:T(8,128)(2,1)}), bf16[16,16,32,128]{3,2,1,0:T(8,128)(2,1)S(1)}, u32[]{:S(2)}, u32[]{:S(2)}) async-start(bf16[16,16,32,128]{3,2,1,0:T(8,128)(2,1)} %to_modes.4), calls=%async_computation.6 | async-start | bytes 4194304 | tf_op jit(solution)/shard_map/all_to_all | solution.py:424
  1121.8 15.8 %copy-start.5 = (bf16[128,128]{1,0:T(8,128)(2,1)S(1)}, bf16[128,128]{1,0:T(8,128)(2,1)}, u32[]{:S(2)}) copy-start(bf16[128,128]{1,0:T(8,128)(2,1)} %param.15) | copy-start | bytes 98308
  1121.8 16.5 %copy-start.6 = (bf16[128,128]{1,0:T(8,128)(2,1)S(1)}, bf16[128,128]{1,0:T(8,128)(2,1)}, u32[]{:S(2)}) copy-start(bf16[128,128]{1,0:T(8,128)(2,1)} %param.16) | copy-start | bytes 98308
  1171.1 1.3 copy-start.2

commit v3 on v2

--- a/solution.py
+++ b/solution.py
@@ -12,11 +12,14 @@
 horizontal_scale = 4.0
 VMEM_BYTES = 56 * 2**20
 MAIN_CUTS = (1, 3)
-LAST_CUTS = (3, 1)
 
 
 def params():
     return pltpu.CompilerParams(vmem_limit_bytes=VMEM_BYTES)
+
+
+def padded(count):
+    return (count // 8 + 2) * 8
 
 
 def cost(flops, nbytes):
@@ -117,9 +120,9 @@
 def tile_kernel(
     first, split, unit, pos_ref, low_ref, s_ref, x_ref, *refs
 ):
-    outs = refs[-4 - split : -4]
-    low_side, high_side, rows, scratch = refs[-4:]
-    _, _, n_slots, n_levels = s_ref.shape
+    outs = refs[-5 - split : -5]
+    low_side, high_side, rows, scratch, turned = refs[-5:]
+    _, n_slots, _, n_levels = s_ref.shape
     n_orders = n_slots - 1
     half = n_orders // 2
     pairs, lanes = x_ref.shape[1:]
@@ -131,12 +134,14 @@
     def _():
         for p in range(unit):
             edge = n_orders - low_ref[pos_ref[0] + begin + p]
+            turned[0 : 2 * n_slots] = s_ref[p].astype(jnp.float32).reshape(2 * n_slots, n_levels)
             for c in range(2):
-                low, high = split_orders(s_ref[p, c].astype(jnp.float32), edge, half)
+                coeffs = turned[pl.ds(c, n_slots, stride=2), :]
+                low, high = split_orders(coeffs, edge, half)
                 low_side[p, :, c * n_levels : (c + 1) * n_levels] = low
                 high_side[p, :, c * n_levels : (c + 1) * n_levels] = high
 
-    rows[...] = x_ref[...].astype(jnp.float32).reshape(n_slots * pairs, lanes)
+    rows[0 : n_slots * pairs] = x_ref[...].astype(jnp.float32).reshape(n_slots * pairs, lanes)
     ids = lax.broadcasted_iota(jnp.int32, (half, lanes), 0)
     for p in range(unit):
         body = rows[pl.ds(inside + p, n_orders, stride=pairs), :]
@@ -160,7 +165,7 @@
 
 
 def synthesize_tiles(pos, pair_low, spectra, table, first, count, unit, n_dest, split, after):
-    _, _, n_slots, n_levels = spectra.shape
+    _, n_slots, _, n_levels = spectra.shape
     n_lat = table.shape[2]
     lat_here = n_lat // n_dest
     lanes, pairs = 128, 8
@@ -177,7 +182,7 @@
             grid=(count // unit, n_lat // lanes),
             in_specs=[
                 pl.BlockSpec(
-                    (unit, 2, n_slots, n_levels), lambda u, t, pos, low: (at + u, 0, 0, 0)
+                    (unit, n_slots, 2, n_levels), lambda u, t, pos, low: (at + u, 0, 0, 0)
                 ),
                 pl.BlockSpec(
                     (n_slots, pairs, lanes),
@@ -195,8 +200,9 @@
             scratch_shapes=[
                 pltpu.VMEM((unit, n_orders, 2 * n_levels), jnp.bfloat16),
                 pltpu.VMEM((unit, n_orders // 2, 2 * n_levels), jnp.bfloat16),
-                pltpu.VMEM((n_slots * pairs, lanes), jnp.float32),
+                pltpu.VMEM((padded(n_slots) * pairs, lanes), jnp.float32),
                 pltpu.VMEM((lanes * kl, n_levels), jnp.float32),
+                pltpu.VMEM((2 * padded(n_slots), n_levels), jnp.float32),
             ],
         ),
         out_shape=[jax.ShapeDtypeStruct(out_shape, jnp.bfloat16)] * split,
@@ -294,7 +300,7 @@
 def finish_kernel(
     first, split, pos_ref, low_ref, l_ref, s_ref, to_ref, from_ref, decay_ref, *refs
 ):
-    m_refs, (out_ref, scratch) = refs[:split], refs[-2:]
+    m_refs, (out_ref, scratch, turned) = refs[:split], refs[-3:]
     n_levels = m_refs[0].shape[3]
     n_lat = l_ref.shape[2]
     n_slots = l_ref.shape[1]
@@ -319,12 +325,15 @@
     degree = jnp.where(slots < edge, slots + low, slots - 1).astype(jnp.float32)
     factor = 1.0 + horizontal_scale * degree * (degree + 1.0) / float(n_orders * n_orders)
     factor = factor + decay_ref[...]
+    turned[0 : 2 * n_slots] = s_ref[0].astype(jnp.float32).reshape(2 * n_slots, n_levels)
+    spectra = [turned[pl.ds(c, n_slots, stride=2), :] for c in range(2)]
     for c in range(2):
         nonlinear = scratch[:, c * n_levels : (c + 1) * n_levels]
-        right = s_ref[0, c].astype(jnp.float32) + time_step * nonlinear
+        right = spectra[c] + time_step * nonlinear
         eigen = dot(right.astype(jnp.bfloat16), to_ref[...])
         scaled = (eigen / factor).astype(jnp.bfloat16)
-        out_ref[0, c] = dot(scaled, from_ref[...]).astype(jnp.bfloat16)
+        turned[pl.ds(c, n_slots, stride=2), :] = dot(scaled, from_ref[...])
+    out_ref[0] = turned[0 : 2 * n_slots].reshape(n_slots, 2, n_levels).astype(jnp.bfloat16)
 
 
 def finish(pos, pair_low, modes, table, spectra, to_t, from_t, decay, first, count, out):
@@ -338,7 +347,7 @@
         for begin, x in modes
     ]
     modes = [x for _, x in modes]
-    pair_spec = pl.BlockSpec((1, 2, n_slots, n_levels), lambda p, pos, low: (first + p, 0, 0, 0))
+    pair_spec = pl.BlockSpec((1, n_slots, 2, n_levels), lambda p, pos, low: (first + p, 0, 0, 0))
     square = pl.BlockSpec((n_levels, n_levels), lambda p, pos, low: (0, 0))
     in_specs = [
         pl.BlockSpec((1, n_slots, n_lat), lambda p, pos, low: (first + p, 0, 0)),
@@ -363,7 +372,10 @@
             grid=(count,),
             in_specs=in_specs,
             out_specs=pair_spec,
-            scratch_shapes=[pltpu.VMEM((n_slots, 2 * n_levels), jnp.float32)],
+            scratch_shapes=[
+                pltpu.VMEM((n_slots, 2 * n_levels), jnp.float32),
+                pltpu.VMEM((2 * padded(n_slots), n_levels), jnp.float32),
+            ],
         ),
         out_shape=jax.ShapeDtypeStruct(spectra.shape, jnp.bfloat16),
         input_output_aliases=aliases,
@@ -416,8 +428,8 @@
     unit = min(4, pairs_here)
     units = pairs_here // unit
     main_cuts = cut_units(units, unit, MAIN_CUTS)
-    last_cuts = cut_units(units, unit, LAST_CUTS)
     whole = [(0, pairs_here)]
+    last_cuts = [(0, pairs_here - 2), (pairs_here - 2, 2)] if pairs_here > 4 else whole
     split = 2 if lat_here % 32 == 0 else 1
 
     def exchange(x):
@@ -425,14 +437,13 @@
 
     tiles = pairs_here % 8 == 0 and 128 % lat_here == 0
 
+    slots_ahead = jnp.transpose(spectra, (0, 2, 1, 3))
+
     def lat_functions(rows, first, count, parts, after):
         if tiles:
-            body, rows = synthesize_tiles, jnp.transpose(rows, (1, 0, 2))
+            body, own, rows = synthesize_tiles, slots_ahead, jnp.transpose(rows, (1, 0, 2))
         else:
-            body = synthesize
-        own = spectra
-        if first == 0 and count == unit:
-            own = lax.slice_in_dim(spectra, 0, unit)
+            body, own = synthesize, spectra
         return body(pos, pair_low, own, rows, first, count, unit, n_dest, parts, after)
 
     main_lat = []
@@ -468,7 +479,7 @@
         pieces = []
         for first, count in last_cuts if part == split - 1 else whole:
             rows = rows_of(analysis_table, [(first, count)])
-            modes = to_modes(rows, product, weights, n_dest, n_levels, part, [])
+            modes = to_modes(rows, product, weights, n_dest, n_levels, part, [legendre])
             pieces.append((first, exchange(modes)))
         arrived.append(pieces)
 
@@ -481,7 +492,7 @@
             pair_low,
             modes,
             legendre,
-            spectra,
+            slots_ahead,
             to_t,
             from_t,
             decay,
@@ -489,7 +500,7 @@
             count,
             out,
         )
-    return out
+    return jnp.transpose(out, (0, 2, 1, 3))
 
 
 def solution(mesh):

time: 1200 us -> 1180 us (0.983)
  local copies, waits for them, and re-layouts: 63.5 us -> 47.6 us
    unnamed x22 -> x17, local copies, waits for them, and re-layouts: 24.1 us -> 19.1 us
  transfers between devices with their start and end apart: 6 -> 6, of which waited for: 5 -> 5; matrix products, arithmetic and copies ran while one was open for 5% -> 5% of each run, Pallas kernels for 18% -> 19%
where the time goes in v3:
time: 1180 us; the launch traced here: 1170 us
  blocking collectives  468 us (40%)
  waiting for transfers between devices  381 us (32%)
  Pallas kernels  231 us (20%)
  local copies, waits for them, and re-layouts  47.6 us (4%)
  starting transfers between devices  31 us (3%)
  other arithmetic  14 us (1%)
    all_to_all x2, blocking collectives, exchange(): lax.all_to_all(x, ('ma', 'row'), split_axis=0, concat_axis=0, tiled=True)  468 us
    all_to_all x5, waiting for transfers between devices, exchange(): lax.all_to_all(x, ('ma', 'row'), split_axis=0, concat_axis=0, tiled=True)  381 us
    pallas_call x3, Pallas kernels, synthesize_tiles(): pl.pallas_call(functools.partial(tile_kernel, first, split, unit), grid_s...  98.3 us
    pallas_call x3, Pallas kernels, to_grid(): pl.pallas_call(body, grid=(lat_here // step,), in_specs=first_specs + chu...  63.4 us
    pallas_call x3, Pallas kernels, to_modes(): pl.pallas_call(modes_kernel, grid=(lat_here // step,), in_specs=[pl.Block...  39.9 us
    pallas_call x2, Pallas kernels, finish(): pl.pallas_call(functools.partial(finish_kernel, first, len(modes)), grid_...  29.4 us
    all_to_all x5, starting transfers between devices, exchange(): lax.all_to_all(x, ('ma', 'row'), split_axis=0, concat_axis=0, tiled=True)  24.6 us
  transfers between devices with their start and end apart: 6, of which 5 were waited for; matrix products, arithmetic and copies ran while one was open for 5% of the time, Pallas kernels for 19%

profile of v3, /device:TPU:0, one launch (start us, length us, event | category | flops | bytes accessed | tf_op | source)
XLA Modules:
  0.0 1173.2 jit_solution(486276076271753238)
XLA Ops:
  0.0 0.8 all_to_all.37
  0.9 0.7 reshape.99
  1.6 6.3 all-to-all-start.2
  7.9 13.6 %synthesize_tiles.3.refs_0_ = bf16[16,64,16,128]{3,2,1,0:T(8,128)(2,1)} custom-call(s32[1]{0:T(128)} %bitcast.pos_ref, s32[256]{0:T(256)} %low_ref.9, bf16[16,513,2,128]{3,2,1,0:T(2,128)(2,1)} %bitcast.31, bf16[513,16,1024]{2,1,0:T(8,128)(2,1)} %bitcast.29), custom_call_target="tpu_custom_call" | custom-call | flops 1613758464 | bytes 12599296 | tf_op jit(solution)/shard_map/synthesize_tiles/pallas_call | solution.py:178
  21.5 0.0 all-to-all-done.2
  21.5 6.2 all-to-all-start
  27.7 36.8 %synthesize_tiles.4.refs_0_ = bf16[16,64,48,128]{3,2,1,0:T(8,128)(2,1)} custom-call(s32[1]{0:T(128)} %bitcast.pos_ref, s32[256]{0:T(256)} %low_ref.9, bf16[16,513,2,128]{3,2,1,0:T(2,128)(2,1)} %bitcast.32, bf16[513,16,1024]{2,1,0:T(8,128)(2,1)} %bitcast.30, bf16[16,64,16,128]{3,2,1,0:T(8,128)(2,1)} %synthesize_tiles.3.refs_0_), custom_call_target="tpu_custom_call" | custom-call | flops 4841275392 | bytes 37797888 | tf_op jit(solution)/shard_map/synthesize_tiles/pallas_call | solution.py:178
  64.4 48.0 %synthesize_tiles.5 = (bf16[16,32,64,128]{3,2,1,0:T(8,128)(2,1)}, bf16[16,32,64,128]{3,2,1,0:T(8,128)(2,1)}) custom-call(s32[1]{0:T(128)} %bitcast.pos_ref, s32[256]{0:T(256)} %low_ref.9, bf16[16,513,2,128]{3,2,1,0:T(2,128)(2,1)} %bitcast.33, bf16[513,16,1024]{2,1,0:T(8,128)(2,1)} %bitcast.38, bf16[16,64,48,128]{3,2,1,0:T(8,128)(2,1)} %synthesize_tiles.4.refs_0_), custom_call_target="tpu_custom_call" | custom-call | flops 6455033856 | bytes 50397184 | tf_op jit(solution)/shard_map/synthesize_tiles/pallas_call | solution.py:178
  112.4 9.7 all-to-all-done.refs_0_
  122.1 0.0 copy-start
  122.1 190.3 %all_to_all.54.refs_0_ = bf16[16,32,64,128]{3,2,1,0:T(8,128)(2,1)} all-to-all(bf16[16,32,64,128]{3,2,1,0:T(8,128)(2,1)} %get-tuple-element.8), channel_id=1, replica_groups=mesh['grp'=2,'ma'=4,'row'=4] {'ma','row'}, dimensions={0} | all-to-all | bytes 16777216 | tf_op jit(solution)/shard_map/all_to_all | solution.py:436
  312.4 0.0 copy-done
  312.4 278.0 %all_to_all.55.refs_1_ = bf16[16,64,48,128]{3,2,1,0:T(8,128)(2,1)} all-to-all(bf16[16,64,48,128]{3,2,1,0:T(8,128)(2,1)S(1)} %copy-done), channel_id=1, replica_groups=mesh['grp'=2,'ma'=4,'row'=4] {'ma','row'}, dimensions={0} | all-to-all | bytes 25165824 | tf_op jit(solution)/shard_map/all_to_all | solution.py:436
  590.4 0.0 copy-start.2
  590.4 5.0 all-to-all-start.3
  595.5 0.0 copy-done.2
  595.5 8.3 fusion.6
  603.9 2.1 multiply_convert_fusion
  606.0 2.2 copy.52
  608.1 2.5 convert_element_type.39
  610.6 2.3 convert_element_type.38
  612.9 15.8 %copy.64.refs_0_.l_ref = bf16[16,513,1024]{2,1,0:T(8,128)(2,1)} copy(bf16[16,513,1024]{2,0,1:T(8,128)(2,1)} %param.11) | data formatting | bytes 33619968 | tf_op args[2]
  628.7 0.0 slice-start.1
  628.7 4.1 copy.53
  632.8 0.0 slice-start
  632.8 0.0 slice-done.1
  632.8 1.6 copy.56
  634.4 0.0 slice-done
  634.4 0.2 copy.55
  634.6 3.8 copy.51
  638.3 2.3 convert_element_type.40
  640.6 0.0 copy-start.5
  640.6 2.9 slice.19
  643.5 0.0 copy-done.5
  643.5 0.1 dynamic_slice.3
  643.6 2.9 maximum_bitcast_fusion.table_ref
  646.5 0.5 broadcast.102
  647.1 0.6 reduce
  647.7 0.1 reshape.100
  647.8 0.7 copy.58
  648.5 28.8 %to_grid.3.main_ref = f32[1024,8192]{1,0:T(8,128)} custom-call(bf16[1024,1024]{1,0:T(8,128)(2,1)} %maximum_bitcast_fusion.table_ref, bf16[16,64,16,128]{3,2,1,0:T(8,128)(2,1)} %all-to-all-done.refs_0_, bf16[16,64,48,128]{3,2,1,0:T(8,128)(2,1)} %all_to_all.55.refs_1_), custom_call_target="tpu_custom_call" | custom-call | flops 17179869184 | bytes 50331648 | tf_op jit(solution)/shard_map/to_grid/pallas_call | solution.py:253
  677.3 17.3 %to_grid.5.product_ref = bf16[1024,4096]{1,0:T(8,128)(2,1)} custom-call(bf16[1024,1024]{1,0:T(8,128)(2,1)} %bitcast.36, f32[1024,8192]{1,0:T(8,128)} %to_grid.3.main_ref, f32[1,8192]{1,0:T(1,128)} %bitcast.49, bf16[16,32,64,128]{3,2,1,0:T(8,128)(2,1)} %all_to_all.54.refs_0_), custom_call_target="tpu_custom_call" | custom-call | flops 8589934592 | bytes 25165824 | tf_op jit(solution)/shard_map/to_grid/pallas_call | solution.py:253
  694.6 0.7 broadcast_in_dim.9
  695.3 15.9 %to_modes.5 = bf16[16,56,32,128]{3,2,1,0:T(8,128)(2,1)} custom-call(bf16[896,1024]{1,0:T(8,128)(2,1)} %bitcast.41, bf16[1024,4096]{1,0:T(8,128)(2,1)} %to_grid.5.product_ref, f32[1,8192]{1,0:T(1,128)} %bitcast.42, bf16[16,513,1024]{2,1,0:T(8,128)(2,1)} %copy.64.refs_0_.l_ref), custom_call_target="tpu_custom_call" | custom-call | flops 7516192768 | bytes 15728640 | tf_op jit(solution)/shard_map/to_modes/pallas_call | solution.py:282
  711.2 68.5 %all-to-all-done.3.refs_0_ = bf16[16,32,64,128]{3,2,1,0:T(8,128)(2,1)} async-done(((bf16[16,32,64,128]{3,2,1,0:T(8,128)(2,1)}), bf16[16,32,64,128]{3,2,1,0:T(8,128)(2,1)}, u32[]{:S(2)}, u32[]{:S(2)}) %all-to-all-start.3) | async-done | bytes 8388640 | tf_op jit(solution)/shard_map/all_to_all | solution.py:436
  779.7 5.0 all-to-all-start.7
  784.7 2.2 convert_element_type.36.table_ref
  786.9 17.3 %to_grid.4.product_ref = bf16[1024,4096]{1,0:T(8,128)(2,1)} custom-call(bf16[1024,1024]{1,0:T(8,128)(2,1)} %bitcast.37, f32[1024,8192]{1,0:T(8,128)} %to_grid.3.main_ref, f32[1,8192]{1,0:T(1,128)} %bitcast.50, bf16[16,32,64,128]{3,2,1,0:T(8,128)(2,1)} %all-to-all-done.3.refs_0_), custom_call_target="tpu_custom_call" | custom-call | flops 8589934592 | bytes 25165824 | tf_op jit(solution)/shard_map/to_grid/pallas_call | solution.py:253
  804.2 18.7 %to_modes.3 = bf16[16,64,32,128]{3,2,1,0:T(8,128)(2,1)} custom-call(bf16[1024,1024]{1,0:T(8,128)(2,1)} %convert_element_type.36.table_ref, bf16[1024,4096]{1,0:T(8,128)(2,1)} %to_grid.4.product_ref, f32[1,8192]{1,0:T(1,128)} %bitcast.43, bf16[16,513,1024]{2,1,0:T(8,128)(2,1)} %copy.64.refs_0_.l_ref), custom_call_target="tpu_custom_call" | custom-call | flops 8589934592 | bytes 16777216 | tf_op jit(solution)/shard_map/to_modes/pallas_call | solution.py:282
  822.9 123.6 %all-to-all-done.7.refs_1_ = bf16[16,56,32,128]{3,2,1,0:T(8,128)(2,1)} async-done(((bf16[16,56,32,128]{3,2,1,0:T(8,128)(2,1)}), bf16[16,56,32,128]{3,2,1,0:T(8,128)(2,1)}, u32[]{:S(2)}, u32[]{:S(2)}) %all-to-all-start.7) | async-done | bytes 7340064 | tf_op jit(solution)/shard_map/all_to_all | solution.py:436
  946.5 4.8 all-to-all-start.4
  951.3 1.7 slice_bitcast_fusion.table_ref
  953.0 5.3 to_modes.4
  958.3 0.0 copy-start.3
  958.3 177.2 %all-to-all-done.4.refs_0_ = bf16[16,64,32,128]{3,2,1,0:T(8,128)(2,1)} async-done(((bf16[16,64,32,128]{3,2,1,0:T(8,128)(2,1)}), bf16[16,64,32,128]{3,2,1,0:T(8,128)(2,1)}, u32[]{:S(2)}, u32[]{:S(2)}) %all-to-all-start.4) | async-done | bytes 8388640 | tf_op jit(solution)/shard_map/all_to_all | solution.py:436
  1135.5 3.7 all-to-all-start.6
  1139.2 0.0 copy-done.3
  1139.2 0.7 copy.49
  1139.9 0.0 copy-done.4
  1139.9 0.7 copy.50
  1140.7 23.8 %finish.2.refs_2_ = bf16[16,513,2,128]{3,2,1,0:T(2,128)(2,1)} custom-call(s32[1]{0:T(128)} %bitcast.pos_ref, s32[256]{0:T(256)} %low_ref.9, bf16[16,513,1024]{2,1,0:T(8,128)(2,1)} %copy.64.refs_0_.l_ref, bf16[16,513,2,128]{3,2,1,0:T(2,128)(2,1)} %bitcast.34, bf16[128,128]{1,0:T(8,128)(2,1)} %bitcast.45, bf16[128,128]{1,0:T(8,128)(2,1)} %bitcast.47, ...), custom_call_target="tpu_custom_call" | custom-call | flops 6589513728 | bytes 36743168 | tf_op jit(solution)/shard_map/finish/pallas_call | solution.py:368
  1164.5 1.6 all-to-all-done.6.refs_1_
  1166.1 1.1 copy-done.1
  1167.2 5.6 finish.3
  (5 shorter events, 0.0 us)
Async XLA Ops:
  1.6 19.9 %all-to-all-start.2 = ((f32[4,1,2048]{2,1,0:T(1,128)}), f32[4,1,2048]{2,1,0:T(1,128)S(1)}, u32[]{:S(2)}, u32[]{:S(2)}) async-start(f32[4,1,2048]{2,1,0:T(1,128)} %reshape.99), calls=%async_computation.2 | async-start | bytes 65536 | tf_op jit(solution)/shard_map/all_to_all | solution.py:455
  21.5 100.6 %all-to-all-start = ((bf16[16,64,16,128]{3,2,1,0:T(8,128)(2,1)}), bf16[16,64,16,128]{3,2,1,0:T(8,128)(2,1)}, u32[]{:S(2)}, u32[]{:S(2)}) async-start(bf16[16,64,16,128]{3,2,1,0:T(8,128)(2,1)} %synthesize_tiles.3.refs_0_), calls=%async_computation | async-start | bytes 8388608 | tf_op jit(solution)/shard_map/all_to_all | solution.py:436
  122.1 190.3 %copy-start = (bf16[16,64,48,128]{3,2,1,0:T(8,128)(2,1)S(1)}, bf16[16,64,48,128]{3,2,1,0:T(8,128)(2,1)}, u32[]{:S(2)}) copy-start(bf16[16,64,48,128]{3,2,1,0:T(8,128)(2,1)} %synthesize_tiles.4.refs_0_) | copy-start | bytes 37748740
  590.4 5.1 copy-start.2
  590.4 189.3 %all-to-all-start.3 = ((bf16[16,32,64,128]{3,2,1,0:T(8,128)(2,1)}), bf16[16,32,64,128]{3,2,1,0:T(8,128)(2,1)}, u32[]{:S(2)}, u32[]{:S(2)}) async-start(bf16[16,32,64,128]{3,2,1,0:T(8,128)(2,1)} %get-tuple-element.7), calls=%async_computation.3 | async-start | bytes 16777216 | tf_op jit(solution)/shard_map/all_to_all | solution.py:436
  628.7 4.1 slice-start.1
  632.8 1.6 slice-start
  640.6 2.9 copy-start.5
  779.7 166.8 %all-to-all-start.7 = ((bf16[16,56,32,128]{3,2,1,0:T(8,128)(2,1)}), bf16[16,56,32,128]{3,2,1,0:T(8,128)(2,1)}, u32[]{:S(2)}, u32[]{:S(2)}) async-start(bf16[16,56,32,128]{3,2,1,0:T(8,128)(2,1)} %to_modes.5), calls=%async_computation.7 | async-start | bytes 14680064 | tf_op jit(solution)/shard_map/all_to_all | solution.py:436
  946.5 189.0 %all-to-all-start.4 = ((bf16[16,64,32,128]{3,2,1,0:T(8,128)(2,1)}), bf16[16,64,32,128]{3,2,1,0:T(8,128)(2,1)}, u32[]{:S(2)}, u32[]{:S(2)}) async-start(bf16[16,64,32,128]{3,2,1,0:T(8,128)(2,1)} %to_modes.3), calls=%async_computation.4 | async-start | bytes 16777216 | tf_op jit(solution)/shard_map/all_to_all | solution.py:436
  958.3 180.9 %copy-start.3 = (bf16[128,128]{1,0:T(8,128)(2,1)S(1)}, bf16[128,128]{1,0:T(8,128)(2,1)}, u32[]{:S(2)}) copy-start(bf16[128,128]{1,0:T(8,128)(2,1)} %param.15) | copy-start | bytes 98308
  958.3 181.6 %copy-start.4 = (bf16[128,128]{1,0:T(8,128)(2,1)S(1)}, bf16[128,128]{1,0:T(8,128)(2,1)}, u32[]{:S(2)}) copy-start(bf16[128,128]{1,0:T(8,128)(2,1)} %param.16) | copy-start | bytes 98308
  1135.5 30.6 %all-to-all-start.6 = ((bf16[16,8,32,128]{3,2,1,0:T(8,128)(2,1)}), bf16[16,8,32,128]{3,2,1,0:T(8,128)(2,1)S(1)}, u32[]{:S(2)}, u32[]{:S(2)}) async-start(bf16[16,8,32,128]{3,2,1,0:T(8,128)(2,1)} %to_modes.4), calls=%async_computation.6 | async-start | bytes 2097152 | tf_op jit(solution)/shard_map/all_to_all | solution.py:436
  1166.1 1.1 copy-start.1

commit v4 on v3

--- a/solution.py
+++ b/solution.py
@@ -141,11 +141,20 @@
                 low_side[p, :, c * n_levels : (c + 1) * n_levels] = low
                 high_side[p, :, c * n_levels : (c + 1) * n_levels] = high
 
-    rows[0 : n_slots * pairs] = x_ref[...].astype(jnp.float32).reshape(n_slots * pairs, lanes)
+    n_tiles, _, tile_lanes = rows.shape
+    for tile in range(n_tiles):
+        part = x_ref[:, :, tile * tile_lanes : (tile + 1) * tile_lanes].astype(jnp.float32)
+        rows[tile, 0 : n_slots * pairs] = part.reshape(n_slots * pairs, tile_lanes)
     ids = lax.broadcasted_iota(jnp.int32, (half, lanes), 0)
     for p in range(unit):
-        body = rows[pl.ds(inside + p, n_orders, stride=pairs), :]
-        last = rows[pl.ds(n_orders * pairs + inside + p, 1), :]
+        bodies = [
+            rows[tile, pl.ds(inside + p, n_orders, stride=pairs), :] for tile in range(n_tiles)
+        ]
+        lasts = [
+            rows[tile, pl.ds(n_orders * pairs + inside + p, 1), :] for tile in range(n_tiles)
+        ]
+        body = jnp.concatenate(bodies, axis=1)
+        last = jnp.concatenate(lasts, axis=1)
         upper = jnp.where(ids == 0, last, body[half:]).astype(jnp.bfloat16)
         results = (
             dot(body.astype(jnp.bfloat16), low_side[p], 0, 0),
@@ -168,7 +177,7 @@
     _, n_slots, _, n_levels = spectra.shape
     n_lat = table.shape[2]
     lat_here = n_lat // n_dest
-    lanes, pairs = 128, 8
+    lanes, pairs = 256, 8
     n_orders = n_slots - 1
     kl = 4 * unit
     out_shape = (n_dest, lat_here // split, 4 * count, n_levels)
@@ -200,7 +209,7 @@
             scratch_shapes=[
                 pltpu.VMEM((unit, n_orders, 2 * n_levels), jnp.bfloat16),
                 pltpu.VMEM((unit, n_orders // 2, 2 * n_levels), jnp.bfloat16),
-                pltpu.VMEM((padded(n_slots) * pairs, lanes), jnp.float32),
+                pltpu.VMEM((lanes // 128, padded(n_slots) * pairs, 128), jnp.float32),
                 pltpu.VMEM((lanes * kl, n_levels), jnp.float32),
                 pltpu.VMEM((2 * padded(n_slots), n_levels), jnp.float32),
             ],
@@ -435,7 +444,7 @@
     def exchange(x):
         return lax.all_to_all(x, ("ma", "row"), split_axis=0, concat_axis=0, tiled=True)
 
-    tiles = pairs_here % 8 == 0 and 128 % lat_here == 0
+    tiles = pairs_here % 8 == 0 and 128 % lat_here == 0 and n_lat % 256 == 0
 
     slots_ahead = jnp.transpose(spectra, (0, 2, 1, 3))
 

time: 1180 us -> 1180 us (level)
  Pallas kernels: 231 us -> 215 us
  waiting for transfers between devices: 381 us -> 395 us
    pallas_call x3, Pallas kernels: 98.3 us -> 82.5 us  [synthesize_tiles(): pl.pallas_call(functools.partial(tile_kernel, first, split, unit), grid_s...]
    all_to_all x5, waiting for transfers between devices: 381 us -> 395 us  [exchange(): lax.all_to_all(x, ('ma', 'row'), split_axis=0, concat_axis=0, tiled=True)]
  transfers between devices with their start and end apart: 6 -> 6, of which waited for: 5 -> 5; matrix products, arithmetic and copies ran while one was open for 5% -> 5% of each run, Pallas kernels for 19% -> 18%
where the time goes in v4:
time: 1180 us; the launch traced here: 1170 us
  blocking collectives  468 us (40%)
  waiting for transfers between devices  395 us (33%)
  Pallas kernels  215 us (18%)
  local copies, waits for them, and re-layouts  47.6 us (4%)
  starting transfers between devices  31 us (3%)
  other arithmetic  14 us (1%)
    all_to_all x2, blocking collectives, exchange(): lax.all_to_all(x, ('ma', 'row'), split_axis=0, concat_axis=0, tiled=True)  468 us
    all_to_all x5, waiting for transfers between devices, exchange(): lax.all_to_all(x, ('ma', 'row'), split_axis=0, concat_axis=0, tiled=True)  395 us
    pallas_call x3, Pallas kernels, synthesize_tiles(): pl.pallas_call(functools.partial(tile_kernel, first, split, unit), grid_s...  82.5 us
    pallas_call x3, Pallas kernels, to_grid(): pl.pallas_call(body, grid=(lat_here // step,), in_specs=first_specs + chu...  63.4 us
    pallas_call x3, Pallas kernels, to_modes(): pl.pallas_call(modes_kernel, grid=(lat_here // step,), in_specs=[pl.Block...  39.9 us
    pallas_call x2, Pallas kernels, finish(): pl.pallas_call(functools.partial(finish_kernel, first, len(modes)), grid_...  29.4 us
    all_to_all x5, starting transfers between devices, exchange(): lax.all_to_all(x, ('ma', 'row'), split_axis=0, concat_axis=0, tiled=True)  24.7 us
  transfers between devices with their start and end apart: 6, of which 5 were waited for; matrix products, arithmetic and copies ran while one was open for 5% of the time, Pallas kernels for 18%

profile of v4, /device:TPU:0, one launch (start us, length us, event | category | flops | bytes accessed | tf_op | source)
XLA Modules:
  0.0 1171.6 jit_solution(1424058067697765752)
XLA Ops:
  0.0 0.8 all_to_all.37
  0.9 0.7 reshape.99
  1.6 6.3 all-to-all-start.2
  7.9 11.9 %synthesize_tiles.3.refs_0_ = bf16[16,64,16,128]{3,2,1,0:T(8,128)(2,1)} custom-call(s32[1]{0:T(128)} %bitcast.pos_ref, s32[256]{0:T(256)} %low_ref.9, bf16[16,513,2,128]{3,2,1,0:T(2,128)(2,1)} %bitcast.31, bf16[513,16,1024]{2,1,0:T(8,128)(2,1)} %bitcast.29), custom_call_target="tpu_custom_call" | custom-call | flops 1613758464 | bytes 12599296 | tf_op jit(solution)/shard_map/synthesize_tiles/pallas_call | solution.py:187
  19.8 0.0 all-to-all-done.2
  19.8 6.2 all-to-all-start
  26.0 30.7 %synthesize_tiles.4.refs_0_ = bf16[16,64,48,128]{3,2,1,0:T(8,128)(2,1)} custom-call(s32[1]{0:T(128)} %bitcast.pos_ref, s32[256]{0:T(256)} %low_ref.9, bf16[16,513,2,128]{3,2,1,0:T(2,128)(2,1)} %bitcast.32, bf16[513,16,1024]{2,1,0:T(8,128)(2,1)} %bitcast.30, bf16[16,64,16,128]{3,2,1,0:T(8,128)(2,1)} %synthesize_tiles.3.refs_0_), custom_call_target="tpu_custom_call" | custom-call | flops 4841275392 | bytes 37797888 | tf_op jit(solution)/shard_map/synthesize_tiles/pallas_call | solution.py:187
  56.8 39.8 %synthesize_tiles.5 = (bf16[16,32,64,128]{3,2,1,0:T(8,128)(2,1)}, bf16[16,32,64,128]{3,2,1,0:T(8,128)(2,1)}) custom-call(s32[1]{0:T(128)} %bitcast.pos_ref, s32[256]{0:T(256)} %low_ref.9, bf16[16,513,2,128]{3,2,1,0:T(2,128)(2,1)} %bitcast.33, bf16[513,16,1024]{2,1,0:T(8,128)(2,1)} %bitcast.38, bf16[16,64,48,128]{3,2,1,0:T(8,128)(2,1)} %synthesize_tiles.4.refs_0_), custom_call_target="tpu_custom_call" | custom-call | flops 6455033856 | bytes 50397184 | tf_op jit(solution)/shard_map/synthesize_tiles/pallas_call | solution.py:187
  96.6 23.8 %all-to-all-done.refs_0_ = bf16[16,64,16,128]{3,2,1,0:T(8,128)(2,1)} async-done(((bf16[16,64,16,128]{3,2,1,0:T(8,128)(2,1)}), bf16[16,64,16,128]{3,2,1,0:T(8,128)(2,1)}, u32[]{:S(2)}, u32[]{:S(2)}) %all-to-all-start) | async-done | bytes 4194336 | tf_op jit(solution)/shard_map/all_to_all | solution.py:445
  120.5 0.0 copy-start
  120.5 190.3 %all_to_all.54.refs_0_ = bf16[16,32,64,128]{3,2,1,0:T(8,128)(2,1)} all-to-all(bf16[16,32,64,128]{3,2,1,0:T(8,128)(2,1)} %get-tuple-element.8), channel_id=1, replica_groups=mesh['grp'=2,'ma'=4,'row'=4] {'ma','row'}, dimensions={0} | all-to-all | bytes 16777216 | tf_op jit(solution)/shard_map/all_to_all | solution.py:445
  310.8 0.0 copy-done
  310.8 278.0 %all_to_all.55.refs_1_ = bf16[16,64,48,128]{3,2,1,0:T(8,128)(2,1)} all-to-all(bf16[16,64,48,128]{3,2,1,0:T(8,128)(2,1)S(1)} %copy-done), channel_id=1, replica_groups=mesh['grp'=2,'ma'=4,'row'=4] {'ma','row'}, dimensions={0} | all-to-all | bytes 25165824 | tf_op jit(solution)/shard_map/all_to_all | solution.py:445
  588.8 0.0 copy-start.2
  588.8 5.0 all-to-all-start.3
  593.9 0.0 copy-done.2
  593.9 8.3 fusion.6
  602.3 2.1 multiply_convert_fusion
  604.3 2.2 copy.52
  606.5 2.5 convert_element_type.39
  609.0 2.3 convert_element_type.38
  611.2 15.8 %copy.64.refs_0_.l_ref = bf16[16,513,1024]{2,1,0:T(8,128)(2,1)} copy(bf16[16,513,1024]{2,0,1:T(8,128)(2,1)} %param.11) | data formatting | bytes 33619968 | tf_op args[2]
  627.1 0.0 slice-start.1
  627.1 4.1 copy.53
  631.2 0.0 slice-start
  631.2 0.0 slice-done.1
  631.2 1.6 copy.56
  632.8 0.0 slice-done
  632.8 0.2 copy.55
  633.0 3.8 copy.51
  636.7 2.3 convert_element_type.40
  639.0 0.0 copy-start.5
  639.0 2.9 slice.19
  641.9 0.0 copy-done.5
  641.9 0.1 dynamic_slice.3
  642.0 2.9 maximum_bitcast_fusion.table_ref
  644.9 0.5 broadcast.102
  645.4 0.6 reduce
  646.1 0.1 reshape.100
  646.2 0.7 copy.58
  646.9 28.8 %to_grid.3.main_ref = f32[1024,8192]{1,0:T(8,128)} custom-call(bf16[1024,1024]{1,0:T(8,128)(2,1)} %maximum_bitcast_fusion.table_ref, bf16[16,64,16,128]{3,2,1,0:T(8,128)(2,1)} %all-to-all-done.refs_0_, bf16[16,64,48,128]{3,2,1,0:T(8,128)(2,1)} %all_to_all.55.refs_1_), custom_call_target="tpu_custom_call" | custom-call | flops 17179869184 | bytes 50331648 | tf_op jit(solution)/shard_map/to_grid/pallas_call | solution.py:262
  675.7 17.3 %to_grid.5.product_ref = bf16[1024,4096]{1,0:T(8,128)(2,1)} custom-call(bf16[1024,1024]{1,0:T(8,128)(2,1)} %bitcast.36, f32[1024,8192]{1,0:T(8,128)} %to_grid.3.main_ref, f32[1,8192]{1,0:T(1,128)} %bitcast.49, bf16[16,32,64,128]{3,2,1,0:T(8,128)(2,1)} %all_to_all.54.refs_0_), custom_call_target="tpu_custom_call" | custom-call | flops 8589934592 | bytes 25165824 | tf_op jit(solution)/shard_map/to_grid/pallas_call | solution.py:262
  693.0 0.7 broadcast_in_dim.9
  693.7 15.9 %to_modes.5 = bf16[16,56,32,128]{3,2,1,0:T(8,128)(2,1)} custom-call(bf16[896,1024]{1,0:T(8,128)(2,1)} %bitcast.41, bf16[1024,4096]{1,0:T(8,128)(2,1)} %to_grid.5.product_ref, f32[1,8192]{1,0:T(1,128)} %bitcast.42, bf16[16,513,1024]{2,1,0:T(8,128)(2,1)} %copy.64.refs_0_.l_ref), custom_call_target="tpu_custom_call" | custom-call | flops 7516192768 | bytes 15728640 | tf_op jit(solution)/shard_map/to_modes/pallas_call | solution.py:291
  709.6 68.5 %all-to-all-done.3.refs_0_ = bf16[16,32,64,128]{3,2,1,0:T(8,128)(2,1)} async-done(((bf16[16,32,64,128]{3,2,1,0:T(8,128)(2,1)}), bf16[16,32,64,128]{3,2,1,0:T(8,128)(2,1)}, u32[]{:S(2)}, u32[]{:S(2)}) %all-to-all-start.3) | async-done | bytes 8388640 | tf_op jit(solution)/shard_map/all_to_all | solution.py:445
  778.1 5.0 all-to-all-start.7
  783.1 2.2 convert_element_type.36.table_ref
  785.3 17.3 %to_grid.4.product_ref = bf16[1024,4096]{1,0:T(8,128)(2,1)} custom-call(bf16[1024,1024]{1,0:T(8,128)(2,1)} %bitcast.37, f32[1024,8192]{1,0:T(8,128)} %to_grid.3.main_ref, f32[1,8192]{1,0:T(1,128)} %bitcast.50, bf16[16,32,64,128]{3,2,1,0:T(8,128)(2,1)} %all-to-all-done.3.refs_0_), custom_call_target="tpu_custom_call" | custom-call | flops 8589934592 | bytes 25165824 | tf_op jit(solution)/shard_map/to_grid/pallas_call | solution.py:262
  802.6 18.7 %to_modes.3 = bf16[16,64,32,128]{3,2,1,0:T(8,128)(2,1)} custom-call(bf16[1024,1024]{1,0:T(8,128)(2,1)} %convert_element_type.36.table_ref, bf16[1024,4096]{1,0:T(8,128)(2,1)} %to_grid.4.product_ref, f32[1,8192]{1,0:T(1,128)} %bitcast.43, bf16[16,513,1024]{2,1,0:T(8,128)(2,1)} %copy.64.refs_0_.l_ref), custom_call_target="tpu_custom_call" | custom-call | flops 8589934592 | bytes 16777216 | tf_op jit(solution)/shard_map/to_modes/pallas_call | solution.py:291
  821.3 123.6 %all-to-all-done.7.refs_1_ = bf16[16,56,32,128]{3,2,1,0:T(8,128)(2,1)} async-done(((bf16[16,56,32,128]{3,2,1,0:T(8,128)(2,1)}), bf16[16,56,32,128]{3,2,1,0:T(8,128)(2,1)}, u32[]{:S(2)}, u32[]{:S(2)}) %all-to-all-start.7) | async-done | bytes 7340064 | tf_op jit(solution)/shard_map/all_to_all | solution.py:445
  944.9 4.8 all-to-all-start.4
  949.7 1.7 slice_bitcast_fusion.table_ref
  951.3 5.3 to_modes.4
  956.7 0.0 copy-start.3
  956.7 177.2 %all-to-all-done.4.refs_0_ = bf16[16,64,32,128]{3,2,1,0:T(8,128)(2,1)} async-done(((bf16[16,64,32,128]{3,2,1,0:T(8,128)(2,1)}), bf16[16,64,32,128]{3,2,1,0:T(8,128)(2,1)}, u32[]{:S(2)}, u32[]{:S(2)}) %all-to-all-start.4) | async-done | bytes 8388640 | tf_op jit(solution)/shard_map/all_to_all | solution.py:445
  1133.9 3.7 all-to-all-start.6
  1137.6 0.0 copy-done.3
  1137.6 0.7 copy.49
  1138.3 0.0 copy-done.4
  1138.3 0.7 copy.50
  1139.0 23.8 %finish.2.refs_2_ = bf16[16,513,2,128]{3,2,1,0:T(2,128)(2,1)} custom-call(s32[1]{0:T(128)} %bitcast.pos_ref, s32[256]{0:T(256)} %low_ref.9, bf16[16,513,1024]{2,1,0:T(8,128)(2,1)} %copy.64.refs_0_.l_ref, bf16[16,513,2,128]{3,2,1,0:T(2,128)(2,1)} %bitcast.34, bf16[128,128]{1,0:T(8,128)(2,1)} %bitcast.45, bf16[128,128]{1,0:T(8,128)(2,1)} %bitcast.47, ...), custom_call_target="tpu_custom_call" | custom-call | flops 6589513728 | bytes 36743168 | tf_op jit(solution)/shard_map/finish/pallas_call | solution.py:377
  1162.9 1.6 all-to-all-done.6.refs_1_
  1164.5 1.1 copy-done.1
  1165.6 5.6 finish.3
  (5 shorter events, 0.0 us)
Async XLA Ops:
  1.6 18.3 %all-to-all-start.2 = ((f32[4,1,2048]{2,1,0:T(1,128)}), f32[4,1,2048]{2,1,0:T(1,128)S(1)}, u32[]{:S(2)}, u32[]{:S(2)}) async-start(f32[4,1,2048]{2,1,0:T(1,128)} %reshape.99), calls=%async_computation.2 | async-start | bytes 65536 | tf_op jit(solution)/shard_map/all_to_all | solution.py:464
  19.8 100.7 %all-to-all-start = ((bf16[16,64,16,128]{3,2,1,0:T(8,128)(2,1)}), bf16[16,64,16,128]{3,2,1,0:T(8,128)(2,1)}, u32[]{:S(2)}, u32[]{:S(2)}) async-start(bf16[16,64,16,128]{3,2,1,0:T(8,128)(2,1)} %synthesize_tiles.3.refs_0_), calls=%async_computation | async-start | bytes 8388608 | tf_op jit(solution)/shard_map/all_to_all | solution.py:445
  120.5 190.3 %copy-start = (bf16[16,64,48,128]{3,2,1,0:T(8,128)(2,1)S(1)}, bf16[16,64,48,128]{3,2,1,0:T(8,128)(2,1)}, u32[]{:S(2)}) copy-start(bf16[16,64,48,128]{3,2,1,0:T(8,128)(2,1)} %synthesize_tiles.4.refs_0_) | copy-start | bytes 37748740
  588.8 5.1 copy-start.2
  588.8 189.3 %all-to-all-start.3 = ((bf16[16,32,64,128]{3,2,1,0:T(8,128)(2,1)}), bf16[16,32,64,128]{3,2,1,0:T(8,128)(2,1)}, u32[]{:S(2)}, u32[]{:S(2)}) async-start(bf16[16,32,64,128]{3,2,1,0:T(8,128)(2,1)} %get-tuple-element.7), calls=%async_computation.3 | async-start | bytes 16777216 | tf_op jit(solution)/shard_map/all_to_all | solution.py:445
  627.1 4.1 slice-start.1
  631.2 1.6 slice-start
  639.0 2.9 copy-start.5
  778.1 166.8 %all-to-all-start.7 = ((bf16[16,56,32,128]{3,2,1,0:T(8,128)(2,1)}), bf16[16,56,32,128]{3,2,1,0:T(8,128)(2,1)}, u32[]{:S(2)}, u32[]{:S(2)}) async-start(bf16[16,56,32,128]{3,2,1,0:T(8,128)(2,1)} %to_modes.5), calls=%async_computation.7 | async-start | bytes 14680064 | tf_op jit(solution)/shard_map/all_to_all | solution.py:445
  944.9 189.0 %all-to-all-start.4 = ((bf16[16,64,32,128]{3,2,1,0:T(8,128)(2,1)}), bf16[16,64,32,128]{3,2,1,0:T(8,128)(2,1)}, u32[]{:S(2)}, u32[]{:S(2)}) async-start(bf16[16,64,32,128]{3,2,1,0:T(8,128)(2,1)} %to_modes.3), calls=%async_computation.4 | async-start | bytes 16777216 | tf_op jit(solution)/shard_map/all_to_all | solution.py:445
  956.7 180.9 %copy-start.3 = (bf16[128,128]{1,0:T(8,128)(2,1)S(1)}, bf16[128,128]{1,0:T(8,128)(2,1)}, u32[]{:S(2)}) copy-start(bf16[128,128]{1,0:T(8,128)(2,1)} %param.15) | copy-start | bytes 98308
  956.7 181.6 %copy-start.4 = (bf16[128,128]{1,0:T(8,128)(2,1)S(1)}, bf16[128,128]{1,0:T(8,128)(2,1)}, u32[]{:S(2)}) copy-start(bf16[128,128]{1,0:T(8,128)(2,1)} %param.16) | copy-start | bytes 98308
  1133.9 30.6 %all-to-all-start.6 = ((bf16[16,8,32,128]{3,2,1,0:T(8,128)(2,1)}), bf16[16,8,32,128]{3,2,1,0:T(8,128)(2,1)S(1)}, u32[]{:S(2)}, u32[]{:S(2)}) async-start(bf16[16,8,32,128]{3,2,1,0:T(8,128)(2,1)} %to_modes.4), calls=%async_computation.6 | async-start | bytes 2097152 | tf_op jit(solution)/shard_map/all_to_all | solution.py:445
  1164.5 1.1 copy-start.1
